TPU v7x, 32 devices: a whole 2x2x4 slice. The times are simulated.
32 devices in a mesh: groups: 2 (over y), coord: 16 (over z, x, core).
Axes of the slice: x: 2, y: 2, z: 4, core: 2. Of those that a mesh axis runs over, the one named last changes fastest.
Arguments:
- activations: bfloat16 [64, 128, 4096], P(('groups', 'coord')), parts along dimension 0, may hold values from -6 to 6
- out_grads: bfloat16 [64, 128, 4096], P(('groups', 'coord')), parts along dimension 0, may hold values from -6 to 6
- proj_in: bfloat16 [4096, 128], P('coord'), may hold values from -0.09375 to 0.09375
- proj_out: bfloat16 [4096, 128], P('coord'), may hold values from -0.09375 to 0.09375
- cov_in: float32 [128, 128], replicated
- cov_out: float32 [128, 128], replicated
- lengths: int32 [64], P(('groups', 'coord')), parts along dimension 0, may hold values from 1 to 128
- seq_ids: int32 [64], P(('groups', 'coord')), parts along dimension 0, may hold values from 0 to 31, each once
- bank: bfloat16 [1536, 16384], P(None, 'coord'), may hold values from -0.015625 to 0.015625
Outputs:
- scores: bfloat16 [64, 1536], P('groups', 'coord'), parts along dimension 0
There are 2 independent parts, one for each index of `groups`. A program takes and returns all parts, laid end to end along the dimension named above; an argument that names none is the same for every part. Nothing has to cross between parts.
All inputs are finite; a program needn't handle non-finite values.
Results may differ from a plain program's by a relative error of at most 0.0064.
Values may be sent and summed in bfloat16 or wider, within the bound.
No kernel may reach another device: no remote copies, remote signals or barrier semaphores. Data moves between devices by JAX's collectives and lax.ppermute only.
A program may use at most 128 MiB of HBM per device.

v0:
```python
import functools

import jax
import jax.numpy as jnp
from jax import lax
from jax.experimental import pallas as pl
from jax.experimental.pallas import tpu as pltpu
from jax.sharding import PartitionSpec as P

SUB = 8
LANES = 128
EXACT = lax.Precision.HIGHEST
VMEM = pl.BlockSpec(memory_space=pltpu.VMEM)
HBM = pl.BlockSpec(memory_space=pltpu.HBM)
SMEM = pl.BlockSpec(memory_space=pltpu.SMEM)


def factors(n):
    c = 2 if n % 2 == 0 else 1
    rest = n // c
    b = max(f for f in range(1, rest + 1) if rest % f == 0 and f * f <= rest)
    return rest // b, b, c


def partner(at, by, size, towards):
    if size & (size - 1) == 0:
        return at ^ by
    return (at + (by if towards else size - by)) % size


def sources(me, n):
    a, b, c = factors(n)
    ia, ib, ic = me // (b * c), (me // c) % b, me % c
    return [
        (partner(ia, da, a, False) * b + partner(ib, db, b, False)) * c + partner(ic, dc, c, False)
        for dc in range(c)
        for db in range(b)
        for da in range(a)
    ]


def moved(value, by, n):
    sizes = factors(n)
    a, b, c = sizes
    pairs = []
    for me in range(n):
        at = (me // (b * c), (me // c) % b, me % c)
        to = [partner(place, step, size, True) for place, step, size in zip(at, by, sizes)]
        pairs.append((me, (to[0] * b + to[1]) * c + to[2]))
    return lax.ppermute(value, "coord", pairs)


def pack_kernel(first_hbm, second_hbm, out_ref, sems):
    rows = first_hbm.shape[0]
    copies = [
        pltpu.make_async_copy(source, out_ref.at[pl.ds(i * rows, rows)], sems.at[i])
        for i, source in enumerate((first_hbm, second_hbm))
    ]
    for copy in copies:
        copy.start()
    for copy in copies:
        copy.wait()


def pack(first, second):
    rows, columns = first.shape
    return pl.pallas_call(
        pack_kernel,
        out_shape=jax.ShapeDtypeStruct((2 * rows, columns), first.dtype),
        in_specs=[HBM, HBM],
        out_specs=VMEM,
        scratch_shapes=[pltpu.SemaphoreType.DMA((2,))],
        compiler_params=pltpu.CompilerParams(vmem_limit_bytes=8 << 20),
        name="pack",
    )(pinned(first), pinned(second))


def pinned(value):
    return pltpu.with_memory_space_constraint(value, pltpu.HBM)


def gauss_jordan(blocks):
    width = blocks[0].shape[1]
    half = width // 2
    lane = lax.broadcasted_iota(jnp.int32, (SUB, width), 1)
    sub = lax.broadcasted_iota(jnp.int32, (SUB, width), 0)
    start, within = lane // half * half, lane % half

    def column(block, at):
        return jnp.take_along_axis(block, start + at, axis=1, mode="promise_in_bounds")

    for k in range(len(blocks)):
        at = k * SUB
        head = within // SUB == k
        rows = [jnp.broadcast_to(blocks[k][i : i + 1, :], (SUB, width)) for i in range(SUB)]
        diag = {(i, j): column(rows[i], at + j) for i in range(SUB) for j in range(i, SUB)}
        rows = [jnp.where(head, (within == at + i).astype(jnp.float32), rows[i]) for i in range(SUB)]
        inverse, factor = [], {}
        for p in range(SUB):
            inverse.append(1.0 / diag[p, p])
            for i in range(p + 1, SUB):
                factor[p, i] = diag[p, i] * inverse[p]
                for j in range(i, SUB):
                    diag[i, j] = diag[i, j] - factor[p, i] * diag[p, j]
                rows[i] = rows[i] - factor[p, i] * rows[p]
        rows = [rows[p] * inverse[p] for p in range(SUB)]
        for p in reversed(range(SUB)):
            for i in range(p):
                rows[i] = rows[i] - factor[i, p] * rows[p]
        done = rows[0]
        for i in range(1, SUB):
            done = jnp.where(sub == i, rows[i], done)
        out = []
        for g, block in enumerate(blocks):
            if g == k:
                out.append(done)
                continue
            terms = [column(block, at + p) * rows[p] for p in range(SUB)]
            while len(terms) > 1:
                terms = [terms[i] + terms[i + 1] for i in range(0, len(terms), 2)]
            out.append(jnp.where(head, 0.0, block) - terms[0])
        blocks = out
    return blocks


def side_by_side_inverses(first, second):
    half = first.shape[0]
    both = jnp.concatenate([first, second], axis=1)
    blocks = gauss_jordan([both[g : g + SUB, :] for g in range(0, half, SUB)])
    both = jnp.concatenate(blocks, axis=0)
    return both[:, :half], both[:, half:]


def damped(cov):
    size = cov.shape[0]
    cov = 0.5 * (cov + cov.T)
    row = lax.broadcasted_iota(jnp.int32, (size, size), 0)
    col = lax.broadcasted_iota(jnp.int32, (size, size), 1)
    damping = 0.1 * jnp.sum(jnp.where(row == col, cov, 0.0)) / size
    return jnp.where(row == col, cov + damping, cov)


def product(left, right, dims=((1,), (0,))):
    return lax.dot_general(left, right, (dims, ((), ())), precision=EXACT, preferred_element_type=jnp.float32)


def first_half_kernel(cov_in_hbm, cov_out_hbm, out_ref, cov_ref, sems):
    copies = [
        pltpu.make_async_copy(source, cov_ref.at[i], sems.at[i]) for i, source in enumerate((cov_in_hbm, cov_out_hbm))
    ]
    for copy in copies:
        copy.start()
    for copy in copies:
        copy.wait()
    half = cov_ref.shape[1] // 2
    covs = [damped(cov_ref[0]), damped(cov_ref[1])]
    corner = [cov[:half, half:] for cov in covs]
    upper = side_by_side_inverses(*[cov[:half, :half] for cov in covs])
    solved = [product(u, c) for u, c in zip(upper, corner)]
    schur = [cov[half:, half:] - product(c, t, ((0,), (0,))) for cov, c, t in zip(covs, corner, solved)]
    for i, pair in enumerate((upper, solved, schur)):
        out_ref[i] = jnp.concatenate(pair, axis=1)


def second_half_kernel(first_ref, len_hbm, k_ref, len_ref, sem):
    copy = pltpu.make_async_copy(len_hbm, len_ref, sem)
    copy.start()
    size = k_ref.shape[1]
    half = size // 2
    upper, solved, schur = [(first_ref[i][:, :half], first_ref[i][:, half:]) for i in range(3)]
    lower = side_by_side_inverses(*schur)
    for m, (u, t, low) in enumerate(zip(upper, solved, lower)):
        side = product(t, low)
        k_ref[m, :half, :half] = u + product(side, t, ((1,), (1,)))
        k_ref[m, :half, half:] = -side
        k_ref[m, half:, :half] = -side.T
        k_ref[m, half:, half:] = low
    copy.wait()
    token = lax.broadcasted_iota(jnp.int32, (size, size), 0)
    lane = lax.broadcasted_iota(jnp.int32, (size, size), 1)
    mask = jnp.zeros((size, size), jnp.float32)
    for s in range(len_ref.shape[0]):
        mask = jnp.where((lane == s) & (token < len_ref[s]), 1.0, mask)
    k_ref[2] = mask


def first_half(cov_in, cov_out):
    size = cov_in.shape[0]
    return pl.pallas_call(
        first_half_kernel,
        out_shape=jax.ShapeDtypeStruct((3, size // 2, size), jnp.float32),
        in_specs=[HBM, HBM],
        out_specs=VMEM,
        scratch_shapes=[pltpu.VMEM((2, size, size), jnp.float32), pltpu.SemaphoreType.DMA((2,))],
        compiler_params=pltpu.CompilerParams(vmem_limit_bytes=8 << 20),
        cost_estimate=pl.CostEstimate(flops=size, bytes_accessed=size, transcendentals=0),
        name="first_half",
    )(pinned(cov_in), pinned(cov_out))


def second_half(first, lengths):
    size = first.shape[2]
    return pl.pallas_call(
        second_half_kernel,
        out_shape=jax.ShapeDtypeStruct((3, size, size), jnp.float32),
        in_specs=[VMEM, HBM],
        out_specs=VMEM,
        scratch_shapes=[pltpu.SMEM(lengths.shape, jnp.int32), pltpu.SemaphoreType.DMA],
        compiler_params=pltpu.CompilerParams(vmem_limit_bytes=8 << 20),
        cost_estimate=pl.CostEstimate(flops=size, bytes_accessed=size, transcendentals=0),
        name="second_half",
    )(first, pinned(lengths))


def merge_kernel(spans, *refs):
    at = 0
    for ref, (start, rows) in zip(refs[:-1], spans):
        refs[-1][at : at + rows, :] = ref[start : start + rows, :]
        at += rows


def merge(parts):
    array, start, rows = parts[0]
    if len(parts) == 1 and rows == array.shape[0]:
        return array
    total = sum(part[2] for part in parts)
    return pl.pallas_call(
        functools.partial(merge_kernel, [part[1:] for part in parts]),
        out_shape=jax.ShapeDtypeStruct((total, array.shape[1]), array.dtype),
        in_specs=[VMEM] * len(parts),
        out_specs=VMEM,
        compiler_params=pltpu.CompilerParams(vmem_limit_bytes=16 << 20),
        cost_estimate=pl.CostEstimate(flops=total, bytes_accessed=total, transcendentals=0),
        name="merge",
    )(*(part[0] for part in parts))


def joined(parts):
    out = []
    for array, start, rows in parts:
        if out and out[-1][0] is array and out[-1][1] + out[-1][2] == start:
            out[-1] = (array, out[-1][1], out[-1][2] + rows)
        else:
            out.append((array, start, rows))
    return out


def project_kernel(n, early, seqs, me_ref, *rest):
    inputs, blocks, (total_ref, held, sems) = rest[:2], rest[2 : 2 + len(early)], rest[2 + len(early) :]
    tokens = held.shape[1]
    part = tokens // sems.shape[1]
    copies = [
        [
            pltpu.make_async_copy(source.at[pl.ds(i * part, part)], held.at[t, pl.ds(i * part, part)], sems.at[t, i])
            for i in range(sems.shape[1])
        ]
        for t, source in enumerate(inputs)
    ]
    for copy in copies[0] + copies[1]:
        copy.start()
    rows = blocks[0].shape[0] // 2
    source = sources(me_ref[0], n)
    for t in range(2):
        for copy in copies[t]:
            copy.wait()
        total = None
        for which, block in zip(early, blocks):
            columns = pl.ds(pl.multiple_of(source[which] * rows, rows), rows)
            term = jnp.dot(
                held[t, :, columns], block[t * rows : (t + 1) * rows, :], preferred_element_type=jnp.float32
            )
            total = term if total is None else total + term
        total_ref[t] = total


def project_whole_kernel(n, me_ref, act_ref, grad_ref, *rest):
    blocks, (total_ref, proj) = rest[:n], rest[n:]
    rows = blocks[0].shape[0] // 2
    for block, source in zip(blocks, sources(me_ref[0], n)):
        at = pl.ds(pl.multiple_of(source * rows, rows), rows)
        for t in range(2):
            proj[t, at, :] = block[t * rows : (t + 1) * rows, :]
    for t, ref in enumerate((act_ref, grad_ref)):
        total_ref[t] = jnp.dot(ref[...], proj[t], preferred_element_type=jnp.float32)


def project(me, activations, out_grads, blocks, early, seqs, n):
    tokens, width = activations.shape
    rank = blocks[0].shape[1]
    total = jax.ShapeDtypeStruct((2, tokens, rank), jnp.float32)
    common = dict(
        compiler_params=pltpu.CompilerParams(vmem_limit_bytes=16 << 20),
        cost_estimate=pl.CostEstimate(flops=rank, bytes_accessed=rank, transcendentals=0),
        name="project",
    )
    if len(early) == n:
        result = pl.pallas_call(
            functools.partial(project_whole_kernel, n),
            out_shape=total,
            in_specs=[SMEM] + [VMEM] * (2 + n),
            out_specs=VMEM,
            scratch_shapes=[pltpu.VMEM((2, width, rank), jnp.bfloat16)],
            **common,
        )(me, activations, out_grads, *blocks)
        return result, None
    return pl.pallas_call(
        functools.partial(project_kernel, n, early, seqs),
        out_shape=(
            total,
            jax.ShapeDtypeStruct((2, tokens, width), activations.dtype),
        ),
        in_specs=[SMEM, HBM, HBM] + [VMEM] * len(early),
        out_specs=(VMEM, VMEM),
        scratch_shapes=[pltpu.SemaphoreType.DMA((2, 2 * seqs))],
        **common,
    )(me, pinned(activations), pinned(out_grads), *blocks)


def whiten_kernel(n, seqs, late, me_ref, total_ref, k_ref, *rest):
    operands, (out_ref, white) = rest[:-2], rest[-2:]
    rank = k_ref.shape[1]
    sums = [total_ref[0], total_ref[1]]
    if late:
        held, *blocks = operands
        source = sources(me_ref[0], n)
        rows = held.shape[2] // n
        for which, t, operand, at in late:
            columns = pl.ds(pl.multiple_of(source[which] * rows, rows), rows)
            block = blocks[operand][at : at + rows, :]
            sums[t] = sums[t] + jnp.dot(held[t, :, columns], block, preferred_element_type=jnp.float32)
    length = total_ref.shape[1] // seqs
    share = rank // n
    grads = []
    for s in range(seqs):
        token = slice(s * length, (s + 1) * length)
        x_proj = (sums[0][token, :] * k_ref[2][:length, s : s + 1]).astype(jnp.bfloat16)
        d_proj = sums[1][token, :].astype(jnp.bfloat16)
        grads.append(
            lax.dot_general(d_proj, x_proj, (((0,), (0,)), ((), ())), preferred_element_type=jnp.float32)
        )
    left = product(k_ref[1], jnp.concatenate(grads, axis=1))
    left = jnp.concatenate([left[:, s * rank : (s + 1) * rank] for s in range(seqs)], axis=0)
    full = product(left, k_ref[0])
    for s in range(seqs):
        for d in range(n):
            at = s * rank + d * share
            white[n - 1 - d, s * share : (s + 1) * share, :] = full[at : at + share, :]
    out_ref[...] = white[...].astype(jnp.bfloat16)


def whitened_blocks(me, total, k, late, operands, seqs, n):
    rank = k.shape[1]
    shape = (n, seqs * (rank // n), rank)
    return pl.pallas_call(
        functools.partial(whiten_kernel, n, seqs, late),
        out_shape=jax.ShapeDtypeStruct(shape, jnp.bfloat16),
        in_specs=[SMEM] + [VMEM] * (2 + len(operands)),
        out_specs=VMEM,
        scratch_shapes=[pltpu.VMEM(shape, jnp.float32)],
        compiler_params=pltpu.CompilerParams(vmem_limit_bytes=16 << 20),
        cost_estimate=pl.CostEstimate(flops=64 * rank**3, bytes_accessed=4 << 20, transcendentals=0),
        name="whiten",
    )(me, total, k, *operands)


def exchanged(value, n):
    order = [list(range(n))[::-1]]
    return lax.all_to_all(value, "coord", split_axis=0, concat_axis=0, axis_index_groups=order, tiled=True)


def score_kernel(n, me_ref, ids_ref, white_ref, bank_ref, out_ref, spread):
    seqs = ids_ref.shape[0]
    chunk, rank = white_ref.shape[1:]
    share = chunk // seqs
    total = n * seqs
    spread[...] = white_ref[...].astype(jnp.float32).reshape(n * chunk, rank)
    columns = jnp.concatenate(
        [spread[pl.ds(j, total, stride=share), :].astype(jnp.bfloat16) for j in range(share)], axis=1
    )
    queries = bank_ref.shape[0] // n
    row = lax.broadcasted_iota(jnp.int32, (total, out_ref.shape[2] - queries), 0)
    tail = jnp.zeros(row.shape, jnp.float32)
    for s in range(seqs):
        tail = jnp.where(row == (n - 1 - me_ref[0]) * seqs + s, ids_ref[s].astype(jnp.float32), tail)
    partial = lax.dot_general(
        columns, bank_ref[...], (((1,), (1,)), ((), ())), preferred_element_type=jnp.float32
    )
    for d in range(n):
        at = n - 1 - d
        out_ref[at, :, :queries] = partial[:, d * queries : (d + 1) * queries].astype(out_ref.dtype)
        out_ref[at, :, queries:] = tail.astype(out_ref.dtype)


def partial_scores(me, seq_ids, white, bank):
    n = white.shape[0]
    seqs = seq_ids.shape[0]
    queries = bank.shape[0] // n
    width = (queries // LANES + 1) * LANES
    return pl.pallas_call(
        functools.partial(score_kernel, n),
        out_shape=jax.ShapeDtypeStruct((n, n * seqs, width), jnp.bfloat16),
        in_specs=[SMEM, SMEM, VMEM, VMEM],
        out_specs=VMEM,
        scratch_shapes=[pltpu.VMEM((n * white.shape[1], white.shape[2]), jnp.float32)],
        compiler_params=pltpu.CompilerParams(vmem_limit_bytes=16 << 20),
        cost_estimate=pl.CostEstimate(
            flops=2 * n * seqs * bank.size, bytes_accessed=2 * bank.size, transcendentals=0
        ),
        name="score",
    )(me, seq_ids, white, bank)


def place_kernel(partial_ref, out_ref):
    rows, queries = out_ref.shape
    total = jnp.sum(partial_ref[...].astype(jnp.float32), axis=0)
    raw = total[:, :queries].astype(jnp.bfloat16)
    ids = total[:, queries : queries + 1].astype(jnp.int32)
    chosen = ids == lax.broadcasted_iota(jnp.int32, (rows, rows), 1)
    out_ref[...] = lax.dot_general(
        chosen.astype(jnp.bfloat16), raw, (((0,), (0,)), ((), ())), preferred_element_type=jnp.float32
    ).astype(jnp.bfloat16)


def place(partials, queries):
    return pl.pallas_call(
        lambda a, b: place_kernel(a, b),
        out_shape=jax.ShapeDtypeStruct((partials.shape[1], queries), jnp.bfloat16),
        in_specs=[VMEM],
        out_specs=VMEM,
        compiler_params=pltpu.CompilerParams(vmem_limit_bytes=16 << 20),
        name="place",
    )(partials)


def body(n, activations, out_grads, proj_in, proj_out, cov_in, cov_out, lengths, seq_ids, bank):
    me = lax.axis_index("coord").reshape(1)
    seqs, length, width = activations.shape
    activations, out_grads = activations.reshape(seqs * length, width), out_grads.reshape(seqs * length, width)
    a, b, c = factors(n)
    paired = a & (a - 1) == 0
    packed = pack(proj_in, proj_out)
    half = first_half(cov_in, cov_out)
    held = {(0, 0, 0): packed}
    for at in range(1, min(a, 3)):
        held[at, 0, 0] = moved(packed, (at, 0, 0), n)
    for by in range(1, b):
        held[0, by, 0] = moved(packed, (0, by, 0), n)
    held, half = lax.optimization_barrier((held, half))
    early = list(held)
    rows = proj_in.shape[0]
    halves = {(at, t): (held[at], t * rows, rows) for at in early for t in range(2)}
    wanted = {}
    for at in range(1, a):
        nearest = at & -at
        source = at - nearest if paired and nearest != at else 0
        for by in range(b):
            for t in range(2):
                if ((at, by, 0), t) in halves:
                    continue
                if source or at > 2:
                    wanted[(at, by, 0), t] = (source, 0, 0), (at - source, by, 0)
                elif at == 1 and t == 0:
                    wanted[(at, by, 0), t] = (0, by, 0), (1, 0, 0)
                else:
                    wanted[(at, by, 0), t] = (at, 0, 0), (0, by, 0)
    arrivals = []
    while wanted:
        steps = {}
        for to, (source, step) in wanted.items():
            if (source, to[1]) in halves:
                steps.setdefault(step, []).append((to, source))
        for step, both in steps.items():
            arrived = moved(merge(joined([halves[source, to[1]] for to, source in both])), step, n)
            arrivals.append((arrived, [to for to, _ in both]))
            for i, (to, _) in enumerate(both):
                halves[to] = arrived, i * rows, rows
                del wanted[to]
    k = second_half(half, lengths)
    order = [(at, by, core) for core in range(c) for by in range(b) for at in range(a)]
    if rows % LANES == 0 and arrivals and c == 2:
        total, inputs = project(
            me, activations, out_grads, [held[at] for at in early], [order.index(at) for at in early], seqs, n
        )
        across = [moved(merge([(held[at], 0, 2 * rows) for at in early]), (0, 0, 1), n)]
        waiting, total, k = lax.optimization_barrier(([arrived for arrived, _ in arrivals], total, k))
        across.append(moved(merge([(arrived, 0, arrived.shape[0]) for arrived in waiting]), (0, 0, 1), n))
        operands = [inputs, *across, *waiting]
        late = [
            (order.index(at), t, 2 + i, j * rows)
            for i, (_, group) in enumerate(arrivals)
            for j, (at, t) in enumerate(group)
        ]
        crossed = [[(at, t) for at in early for t in range(2)], [to for _, group in arrivals for to in group]]
        late += [
            (order.index((*at[:2], 1)), t, i, j * rows) for i, part in enumerate(crossed) for j, (at, t) in enumerate(part)
        ]
    else:
        for at in order:
            if at[2] == 0:
                held[at] = merge(joined([halves[at, 0], halves[at, 1]]))
                for by in range(1, c):
                    held[at[0], at[1], by] = moved(held[at], (0, 0, by), n)
        total = project(me, activations, out_grads, [held[at] for at in order], list(range(n)), seqs, n)[0]
        operands, late = [], []
    white = whitened_blocks(me, total, k, late, operands, seqs, n)
    partials = partial_scores(me, seq_ids, exchanged(white, n), bank)
    return place(exchanged(partials, n), bank.shape[0] // n)


def solution(mesh):
    in_specs = (
        P(("groups", "coord"), None, None),
        P(("groups", "coord"), None, None),
        P("coord", None),
        P("coord", None),
        P(),
        P(),
        P(("groups", "coord")),
        P(("groups", "coord")),
        P(None, "coord"),
    )
    out_specs = P("groups", "coord")
    return jax.shard_map(
        functools.partial(body, mesh.shape["coord"]),
        mesh=mesh,
        in_specs=in_specs,
        out_specs=out_specs,
        check_vma=False,
    )
```

profile of v0, /device:TPU:0, one launch (start us, length us, event | category | flops | bytes accessed | tf_op | source)
XLA Modules:
  0.0 48.3 jit_solution(14025964959114590200)
XLA Ops:
  0.0 0.9 %pack.1.rest_2_.refs_0_ = bf16[512,128]{1,0:T(8,128)(2,1)S(1)} custom-call(bf16[256,128]{1,0:T(8,128)(2,1)} %first_hbm.1, bf16[256,128]{1,0:T(8,128)(2,1)} %second_hbm.1), custom_call_target="tpu_custom_call" | custom-call | tf_op jit(solution)/shard_map/pack/pallas_call | solution.py:67
  0.9 4.1 %collective-permute-start.2 = (bf16[512,128]{1,0:T(8,128)(2,1)S(1)}, bf16[512,128]{1,0:T(8,128)(2,1)S(1)}, u32[]{:S(2)}, u32[]{:S(2)}) collective-permute-start(bf16[512,128]{1,0:T(8,128)(2,1)S(1)} %pack.1.rest_2_.refs_0_), channel_id=1, source_target_pairs={{0,8},{1,9},{2,10},{3,11},{4,12},{5,13},{6,14},{7,15},{8,0},{9,1},... | collective-permute-start | bytes 393224 | tf_op jit(solution)/shard_map/ppermute | solution.py:50
  5.0 1.6 %collective-permute-start.1 = (bf16[512,128]{1,0:T(8,128)(2,1)S(1)}, bf16[512,128]{1,0:T(8,128)(2,1)S(1)}, u32[]{:S(2)}, u32[]{:S(2)}) collective-permute-start(bf16[512,128]{1,0:T(8,128)(2,1)S(1)} %pack.1.rest_2_.refs_0_), channel_id=1, source_target_pairs={{0,4},{1,5},{2,6},{3,7},{4,0},{5,1},{6,2},{7,3},{8,12},{9,13},{10,... | collective-permute-start | bytes 393224 | tf_op jit(solution)/shard_map/ppermute | solution.py:50
  6.6 1.5 %collective-permute-start = (bf16[512,128]{1,0:T(8,128)(2,1)S(1)}, bf16[512,128]{1,0:T(8,128)(2,1)S(1)}, u32[]{:S(2)}, u32[]{:S(2)}) collective-permute-start(bf16[512,128]{1,0:T(8,128)(2,1)S(1)} %pack.1.rest_2_.refs_0_), channel_id=1, source_target_pairs={{0,2},{1,3},{2,0},{3,1},{4,6},{5,7},{6,4},{7,5},{8,10},{9,11},{10,... | collective-permute-start | bytes 393224 | tf_op jit(solution)/shard_map/ppermute | solution.py:50
  8.1 4.0 %first_half.1.first_ref = f32[3,64,128]{2,1,0:T(8,128)S(1)} custom-call(f32[128,128]{1,0:T(8,128)} %cov_in_hbm.1, f32[128,128]{1,0:T(8,128)} %cov_out_hbm.1), custom_call_target="tpu_custom_call" | custom-call | flops 128 | bytes 128 | tf_op jit(solution)/shard_map/first_half/pallas_call | solution.py:189
  12.1 0.0 collective-permute-done.2.refs_1_.rest_5_.refs_3_
  12.1 0.0 collective-permute-done.1.refs_0_.rest_4_.refs_2_
  12.1 0.0 collective-permute-done.refs_0_.rest_3_.refs_1_
  12.2 1.1 %collective-permute-start.4 = (bf16[768,128]{1,0:T(8,128)(2,1)S(1)}, bf16[768,128]{1,0:T(8,128)(2,1)S(1)}, u32[]{:S(2)}, u32[]{:S(2)}) collective-permute-start(bf16[768,128]{1,0:T(8,128)(2,1)S(1)} %merge.5), channel_id=1, source_target_pairs={{0,2},{1,3},{2,0},{3,1},{4,6},{5,7},{6,4},{7,5},{8,10},{9,11},{10,... | collective-permute-start | bytes 589832 | tf_op jit(solution)/shard_map/ppermute | solution.py:50
  13.3 1.5 %collective-permute-start.3 = (bf16[768,128]{1,0:T(8,128)(2,1)S(1)}, bf16[768,128]{1,0:T(8,128)(2,1)S(1)}, u32[]{:S(2)}, u32[]{:S(2)}) collective-permute-start(bf16[768,128]{1,0:T(8,128)(2,1)S(1)} %merge.4), channel_id=1, source_target_pairs={{0,4},{1,5},{2,6},{3,7},{4,0},{5,1},{6,2},{7,3},{8,12},{9,13},{10,... | collective-permute-start | bytes 589832 | tf_op jit(solution)/shard_map/ppermute | solution.py:50
  14.7 1.1 %collective-permute-start.5 = (bf16[512,128]{1,0:T(8,128)(2,1)S(1)}, bf16[512,128]{1,0:T(8,128)(2,1)S(1)}, u32[]{:S(2)}, u32[]{:S(2)}) collective-permute-start(bf16[512,128]{1,0:T(8,128)(2,1)S(1)} %collective-permute-done.2.refs_1_.rest_5_.refs_3_), channel_id=1, source_target_pairs={{0,6},{1,7},{2,4},{3,5},{4,2},{5,3},{6,0},{7,1},{8,14},{9,15},{10,... | collective-permute-start | bytes 393224 | tf_op jit(solution)/shard_map/ppermute | solution.py:50
  15.8 0.1 collective-permute-start.6
  15.9 3.2 %second_half.1.k_ref = f32[3,128,128]{2,1,0:T(8,128)S(1)} custom-call(f32[3,64,128]{2,1,0:T(8,128)S(1)} %first_half.1.first_ref, s32[2]{0:T(128)} %len_hbm.1), custom_call_target="tpu_custom_call" | custom-call | flops 128 | bytes 128 | tf_op jit(solution)/shard_map/second_half/pallas_call | solution.py:203
  19.1 2.5 %project.1 = (f32[2,256,128]{2,1,0:T(8,128)S(1)}, bf16[2,256,4096]{2,1,0:T(8,128)(2,1)S(1)}) custom-call(s32[1]{0:T(128)} %bitcast.me_ref, bf16[256,4096]{1,0:T(8,128)(2,1)} %bitcast.3, bf16[256,4096]{1,0:T(8,128)(2,1)} %bitcast.4, bf16[512,128]{1,0:T(8,128)(2,1)S(1)} %pack.1.rest_2_.refs_0_, ...), custom_call_target="tpu_custom_call" | custom-call | flops 128 | bytes 128 | tf_op jit(solution)/shard_map/project/pallas_call | solution.py:306
  21.6 0.5 collective-permute-done.5.refs_2_.rest_5_
  22.1 0.0 collective-permute-done.4.refs_1_.rest_4_
  22.1 0.0 collective-permute-done.3.refs_0_.rest_3_
  22.1 0.1 collective-permute-start.7
  22.3 0.0 collective-permute-done.6.rest_1_
  22.3 1.9 %collective-permute-done.7.rest_2_ = bf16[2048,128]{1,0:T(8,128)(2,1)S(1)} collective-permute-done((bf16[2048,128]{1,0:T(8,128)(2,1)S(1)}, bf16[2048,128]{1,0:T(8,128)(2,1)S(1)}, u32[]{:S(2)}, u32[]{:S(2)}) %collective-permute-start.7) | collective-permute-done | bytes 524320 | tf_op jit(solution)/shard_map/ppermute | solution.py:50
  24.1 0.0 copy-start
  24.1 0.0 copy-start.1
  24.1 1.8 %whiten.1 = bf16[16,16,128]{2,1,0:T(8,128)(2,1)S(1)} custom-call(s32[1]{0:T(128)} %bitcast.me_ref, f32[2,256,128]{2,1,0:T(8,128)S(1)} %get-tuple-element.23.total_ref, f32[3,128,128]{2,1,0:T(8,128)S(1)} %second_half.1.k_ref, bf16[2,256,4096]{2,1,0:T(8,128)(2,1)S(1)} %get-tuple-element.25.rest_0_, bf16[2048,128]{1,0:T(8,128)(2,1)S(1)} %collective-permute-done.6.rest_1_, ...), custom_call_target="tpu_custom_call" | custom-call | flops 134217728 | bytes 4194304 | tf_op jit(solution)/shard_map/whiten/pallas_call | solution.py:354
  25.9 9.7 %all_to_all.10.white_ref = bf16[16,16,128]{2,1,0:T(8,128)(2,1)S(1)} all-to-all(bf16[16,16,128]{2,1,0:T(8,128)(2,1)S(1)} %whiten.1), channel_id=1, replica_groups={{15,14,13,12,11,10,9,8,7,6,5,4,3,2,1,0},{31,30,29,28,27,26,25,24,23,22,..., dimensions={0} | all-to-all | bytes 131072 | tf_op jit(solution)/shard_map/all_to_all | solution.py:368
  35.7 0.0 copy-done
  35.7 0.0 copy-done.1
  35.7 1.7 %score.1 = bf16[16,32,128]{2,1,0:T(8,128)(2,1)S(1)} custom-call(s32[1]{0:T(128)} %bitcast.me_ref, s32[2]{0:T(128)S(1)} %copy-done.1, bf16[16,16,128]{2,1,0:T(8,128)(2,1)S(1)} %all_to_all.10.white_ref, bf16[1536,1024]{1,0:T(8,128)(2,1)S(1)} %copy-done), custom_call_target="tpu_custom_call" | custom-call | flops 100663296 | bytes 3145728 | tf_op jit(solution)/shard_map/score/pallas_call | solution.py:399
  37.4 10.1 %all_to_all.11.a = bf16[16,32,128]{2,1,0:T(8,128)(2,1)S(1)} all-to-all(bf16[16,32,128]{2,1,0:T(8,128)(2,1)S(1)} %score.1), channel_id=1, replica_groups={{15,14,13,12,11,10,9,8,7,6,5,4,3,2,1,0},{31,30,29,28,27,26,25,24,23,22,..., dimensions={0} | all-to-all | bytes 262144 | tf_op jit(solution)/shard_map/all_to_all | solution.py:368
  47.5 0.9 %place.1 = bf16[32,96]{1,0:T(8,128)(2,1)} custom-call(bf16[16,32,128]{2,1,0:T(8,128)(2,1)S(1)} %all_to_all.11.a), custom_call_target="tpu_custom_call" | custom-call | tf_op jit(solution)/shard_map/place/pallas_call | solution.py:425
  (4 shorter events, 0.1 us)
Async XLA Ops:
  0.9 11.2 %collective-permute-start.2 = (bf16[512,128]{1,0:T(8,128)(2,1)S(1)}, bf16[512,128]{1,0:T(8,128)(2,1)S(1)}, u32[]{:S(2)}, u32[]{:S(2)}) collective-permute-start(bf16[512,128]{1,0:T(8,128)(2,1)S(1)} %pack.1.rest_2_.refs_0_), channel_id=1, source_target_pairs={{0,8},{1,9},{2,10},{3,11},{4,12},{5,13},{6,14},{7,15},{8,0},{9,1},... | collective-permute-start | bytes 393224 | tf_op jit(solution)/shard_map/ppermute | solution.py:50
  5.0 7.1 %collective-permute-start.1 = (bf16[512,128]{1,0:T(8,128)(2,1)S(1)}, bf16[512,128]{1,0:T(8,128)(2,1)S(1)}, u32[]{:S(2)}, u32[]{:S(2)}) collective-permute-start(bf16[512,128]{1,0:T(8,128)(2,1)S(1)} %pack.1.rest_2_.refs_0_), channel_id=1, source_target_pairs={{0,4},{1,5},{2,6},{3,7},{4,0},{5,1},{6,2},{7,3},{8,12},{9,13},{10,... | collective-permute-start | bytes 393224 | tf_op jit(solution)/shard_map/ppermute | solution.py:50
  6.6 5.6 %collective-permute-start = (bf16[512,128]{1,0:T(8,128)(2,1)S(1)}, bf16[512,128]{1,0:T(8,128)(2,1)S(1)}, u32[]{:S(2)}, u32[]{:S(2)}) collective-permute-start(bf16[512,128]{1,0:T(8,128)(2,1)S(1)} %pack.1.rest_2_.refs_0_), channel_id=1, source_target_pairs={{0,2},{1,3},{2,0},{3,1},{4,6},{5,7},{6,4},{7,5},{8,10},{9,11},{10,... | collective-permute-start | bytes 393224 | tf_op jit(solution)/shard_map/ppermute | solution.py:50
  12.2 9.9 %collective-permute-start.4 = (bf16[768,128]{1,0:T(8,128)(2,1)S(1)}, bf16[768,128]{1,0:T(8,128)(2,1)S(1)}, u32[]{:S(2)}, u32[]{:S(2)}) collective-permute-start(bf16[768,128]{1,0:T(8,128)(2,1)S(1)} %merge.5), channel_id=1, source_target_pairs={{0,2},{1,3},{2,0},{3,1},{4,6},{5,7},{6,4},{7,5},{8,10},{9,11},{10,... | collective-permute-start | bytes 589832 | tf_op jit(solution)/shard_map/ppermute | solution.py:50
  13.3 8.9 %collective-permute-start.3 = (bf16[768,128]{1,0:T(8,128)(2,1)S(1)}, bf16[768,128]{1,0:T(8,128)(2,1)S(1)}, u32[]{:S(2)}, u32[]{:S(2)}) collective-permute-start(bf16[768,128]{1,0:T(8,128)(2,1)S(1)} %merge.4), channel_id=1, source_target_pairs={{0,4},{1,5},{2,6},{3,7},{4,0},{5,1},{6,2},{7,3},{8,12},{9,13},{10,... | collective-permute-start | bytes 589832 | tf_op jit(solution)/shard_map/ppermute | solution.py:50
  14.7 7.4 %collective-permute-start.5 = (bf16[512,128]{1,0:T(8,128)(2,1)S(1)}, bf16[512,128]{1,0:T(8,128)(2,1)S(1)}, u32[]{:S(2)}, u32[]{:S(2)}) collective-permute-start(bf16[512,128]{1,0:T(8,128)(2,1)S(1)} %collective-permute-done.2.refs_1_.rest_5_.refs_3_), channel_id=1, source_target_pairs={{0,6},{1,7},{2,4},{3,5},{4,2},{5,3},{6,0},{7,1},{8,14},{9,15},{10,... | collective-permute-start | bytes 393224 | tf_op jit(solution)/shard_map/ppermute | solution.py:50
  15.8 6.4 %collective-permute-start.6 = (bf16[2048,128]{1,0:T(8,128)(2,1)S(1)}, bf16[2048,128]{1,0:T(8,128)(2,1)S(1)}, u32[]{:S(2)}, u32[]{:S(2)}) collective-permute-start(bf16[2048,128]{1,0:T(8,128)(2,1)S(1)} %merge.6), channel_id=1, source_target_pairs={{0,1},{1,0},{2,3},{3,2},{4,5},{5,4},{6,7},{7,6},{8,9},{9,8},{10,11... | collective-permute-start | bytes 1572872 | tf_op jit(solution)/shard_map/ppermute | solution.py:50
  22.1 2.0 %collective-permute-start.7 = (bf16[2048,128]{1,0:T(8,128)(2,1)S(1)}, bf16[2048,128]{1,0:T(8,128)(2,1)S(1)}, u32[]{:S(2)}, u32[]{:S(2)}) collective-permute-start(bf16[2048,128]{1,0:T(8,128)(2,1)S(1)} %merge.7), channel_id=1, source_target_pairs={{0,1},{1,0},{2,3},{3,2},{4,5},{5,4},{6,7},{7,6},{8,9},{9,8},{10,11... | collective-permute-start | bytes 1572872 | tf_op jit(solution)/shard_map/ppermute | solution.py:50
  24.1 11.6 %copy-start = (bf16[1536,1024]{1,0:T(8,128)(2,1)S(1)}, bf16[1536,1024]{1,0:T(8,128)(2,1)}, u32[]{:S(2)}) copy-start(bf16[1536,1024]{1,0:T(8,128)(2,1)} %bank_ref.1) | copy-start | bytes 9437188
  24.1 11.6 %copy-start.1 = (s32[2]{0:T(128)S(1)}, s32[2]{0:T(128)}, u32[]{:S(2)}) copy-start(s32[2]{0:T(128)} %ids_ref.1) | copy-start | bytes 28
where the time goes:
time: 48.6 us; the launch traced here: 48.3 us
  blocking collectives  19.8 us (41%)
  Pallas kernels  15.1 us (31%)
  starting transfers between devices  11 us (23%)
  waiting for transfers between devices  2.33 us (5%)
    all_to_all x2, blocking collectives, exchanged(): lax.all_to_all(value, 'coord', split_axis=0, concat_axis=0, axis_index_gr...  19.8 us
    ppermute x8, starting transfers between devices, moved(): return lax.ppermute(value, 'coord', pairs)  11 us
    pallas_call x1, Pallas kernels, first_half(): pl.pallas_call(first_half_kernel, out_shape=jax.ShapeDtypeStruct((3, size...  4.03 us
    pallas_call x1, Pallas kernels, second_half(): pl.pallas_call(second_half_kernel, out_shape=jax.ShapeDtypeStruct((3, siz...  3.19 us
    pallas_call x1, Pallas kernels, project(): pl.pallas_call(functools.partial(project_kernel, n, early, seqs), out_sha...  2.51 us
    ppermute x8, waiting for transfers between devices, moved(): return lax.ppermute(value, 'coord', pairs)  2.33 us
    pallas_call x1, Pallas kernels, whitened_blocks(): pl.pallas_call(functools.partial(whiten_kernel, n, seqs, late), out_shape...  1.8 us
    pallas_call x1, Pallas kernels, partial_scores(): pl.pallas_call(functools.partial(score_kernel, n), out_shape=jax.ShapeDty...  1.66 us
  transfers between devices with their start and end apart: 8, of which 2 were waited for; matrix products, arithmetic and copies ran while one was open for 0% of the time, Pallas kernels for 20%

commit v1 on v0

--- a/solution.py
+++ b/solution.py
@@ -48,6 +48,18 @@
         to = [partner(place, step, size, True) for place, step, size in zip(at, by, sizes)]
         pairs.append((me, (to[0] * b + to[1]) * c + to[2]))
     return lax.ppermute(value, "coord", pairs)
+
+
+def exchange_order(n):
+    a, b, c = factors(n)
+    return sorted(range(n), key=lambda device: (1 - device % 2, abs(2 * (device // (b * c)) - (a - 1)), -device))
+
+
+def place_of(me, n):
+    place = 0
+    for i, device in enumerate(exchange_order(n)):
+        place = jnp.where(me == device, i, place)
+    return place
 
 
 def pack_kernel(first_hbm, second_hbm, out_ref, sems):
@@ -341,10 +353,11 @@
     left = product(k_ref[1], jnp.concatenate(grads, axis=1))
     left = jnp.concatenate([left[:, s * rank : (s + 1) * rank] for s in range(seqs)], axis=0)
     full = product(left, k_ref[0])
+    places = [exchange_order(n).index(d) for d in range(n)]
     for s in range(seqs):
         for d in range(n):
             at = s * rank + d * share
-            white[n - 1 - d, s * share : (s + 1) * share, :] = full[at : at + share, :]
+            white[places[d], s * share : (s + 1) * share, :] = full[at : at + share, :]
     out_ref[...] = white[...].astype(jnp.bfloat16)
 
 
@@ -364,7 +377,7 @@
 
 
 def exchanged(value, n):
-    order = [list(range(n))[::-1]]
+    order = [exchange_order(n)]
     return lax.all_to_all(value, "coord", split_axis=0, concat_axis=0, axis_index_groups=order, tiled=True)
 
 
@@ -380,13 +393,14 @@
     queries = bank_ref.shape[0] // n
     row = lax.broadcasted_iota(jnp.int32, (total, out_ref.shape[2] - queries), 0)
     tail = jnp.zeros(row.shape, jnp.float32)
+    place = place_of(me_ref[0], n)
     for s in range(seqs):
-        tail = jnp.where(row == (n - 1 - me_ref[0]) * seqs + s, ids_ref[s].astype(jnp.float32), tail)
+        tail = jnp.where(row == place * seqs + s, ids_ref[s].astype(jnp.float32), tail)
     partial = lax.dot_general(
         columns, bank_ref[...], (((1,), (1,)), ((), ())), preferred_element_type=jnp.float32
     )
     for d in range(n):
-        at = n - 1 - d
+        at = exchange_order(n).index(d)
         out_ref[at, :, :queries] = partial[:, d * queries : (d + 1) * queries].astype(out_ref.dtype)
         out_ref[at, :, queries:] = tail.astype(out_ref.dtype)
 

time: 48.6 us -> 47.9 us (0.986)
  blocking collectives: 19.8 us -> 19.1 us
    all_to_all x2, blocking collectives: 19.8 us -> 19.1 us  [exchanged(): lax.all_to_all(value, 'coord', split_axis=0, concat_axis=0, axis_index_gr...]
  transfers between devices with their start and end apart: 8 -> 8, of which waited for: 2 -> 2; matrix products, arithmetic and copies ran while one was open for 0% -> 0% of each run, Pallas kernels for 20% -> 21%
where the time goes in v1:
time: 47.9 us; the launch traced here: 47.6 us
  blocking collectives  19.1 us (40%)
  Pallas kernels  15.1 us (32%)
  starting transfers between devices  11 us (23%)
  waiting for transfers between devices  2.33 us (5%)
    all_to_all x2, blocking collectives, exchanged(): lax.all_to_all(value, 'coord', split_axis=0, concat_axis=0, axis_index_gr...  19.1 us
    ppermute x8, starting transfers between devices, moved(): return lax.ppermute(value, 'coord', pairs)  11 us
    pallas_call x1, Pallas kernels, first_half(): pl.pallas_call(first_half_kernel, out_shape=jax.ShapeDtypeStruct((3, size...  4.03 us
    pallas_call x1, Pallas kernels, second_half(): pl.pallas_call(second_half_kernel, out_shape=jax.ShapeDtypeStruct((3, siz...  3.19 us
    pallas_call x1, Pallas kernels, project(): pl.pallas_call(functools.partial(project_kernel, n, early, seqs), out_sha...  2.51 us
    ppermute x8, waiting for transfers between devices, moved(): return lax.ppermute(value, 'coord', pairs)  2.33 us
    pallas_call x1, Pallas kernels, whitened_blocks(): pl.pallas_call(functools.partial(whiten_kernel, n, seqs, late), out_shape...  1.8 us
    pallas_call x1, Pallas kernels, partial_scores(): pl.pallas_call(functools.partial(score_kernel, n), out_shape=jax.ShapeDty...  1.66 us
  transfers between devices with their start and end apart: 8, of which 2 were waited for; matrix products, arithmetic and copies ran while one was open for 0% of the time, Pallas kernels for 21%

profile of v1, /device:TPU:0, one launch (start us, length us, event | category | flops | bytes accessed | tf_op | source)
XLA Modules:
  0.0 47.6 jit_solution(4956788405638587613)
XLA Ops:
  0.0 0.9 %pack.1.rest_2_.refs_0_ = bf16[512,128]{1,0:T(8,128)(2,1)S(1)} custom-call(bf16[256,128]{1,0:T(8,128)(2,1)} %first_hbm.1, bf16[256,128]{1,0:T(8,128)(2,1)} %second_hbm.1), custom_call_target="tpu_custom_call" | custom-call | tf_op jit(solution)/shard_map/pack/pallas_call | solution.py:79
  0.9 4.1 %collective-permute-start.2 = (bf16[512,128]{1,0:T(8,128)(2,1)S(1)}, bf16[512,128]{1,0:T(8,128)(2,1)S(1)}, u32[]{:S(2)}, u32[]{:S(2)}) collective-permute-start(bf16[512,128]{1,0:T(8,128)(2,1)S(1)} %pack.1.rest_2_.refs_0_), channel_id=1, source_target_pairs={{0,8},{1,9},{2,10},{3,11},{4,12},{5,13},{6,14},{7,15},{8,0},{9,1},... | collective-permute-start | bytes 393224 | tf_op jit(solution)/shard_map/ppermute | solution.py:50
  5.0 1.6 %collective-permute-start.1 = (bf16[512,128]{1,0:T(8,128)(2,1)S(1)}, bf16[512,128]{1,0:T(8,128)(2,1)S(1)}, u32[]{:S(2)}, u32[]{:S(2)}) collective-permute-start(bf16[512,128]{1,0:T(8,128)(2,1)S(1)} %pack.1.rest_2_.refs_0_), channel_id=1, source_target_pairs={{0,4},{1,5},{2,6},{3,7},{4,0},{5,1},{6,2},{7,3},{8,12},{9,13},{10,... | collective-permute-start | bytes 393224 | tf_op jit(solution)/shard_map/ppermute | solution.py:50
  6.6 1.5 %collective-permute-start = (bf16[512,128]{1,0:T(8,128)(2,1)S(1)}, bf16[512,128]{1,0:T(8,128)(2,1)S(1)}, u32[]{:S(2)}, u32[]{:S(2)}) collective-permute-start(bf16[512,128]{1,0:T(8,128)(2,1)S(1)} %pack.1.rest_2_.refs_0_), channel_id=1, source_target_pairs={{0,2},{1,3},{2,0},{3,1},{4,6},{5,7},{6,4},{7,5},{8,10},{9,11},{10,... | collective-permute-start | bytes 393224 | tf_op jit(solution)/shard_map/ppermute | solution.py:50
  8.1 4.0 %first_half.1.first_ref = f32[3,64,128]{2,1,0:T(8,128)S(1)} custom-call(f32[128,128]{1,0:T(8,128)} %cov_in_hbm.1, f32[128,128]{1,0:T(8,128)} %cov_out_hbm.1), custom_call_target="tpu_custom_call" | custom-call | flops 128 | bytes 128 | tf_op jit(solution)/shard_map/first_half/pallas_call | solution.py:201
  12.1 0.0 collective-permute-done.2.refs_1_.rest_5_.refs_3_
  12.1 0.0 collective-permute-done.1.refs_0_.rest_4_.refs_2_
  12.1 0.0 collective-permute-done.refs_0_.rest_3_.refs_1_
  12.2 1.1 %collective-permute-start.4 = (bf16[768,128]{1,0:T(8,128)(2,1)S(1)}, bf16[768,128]{1,0:T(8,128)(2,1)S(1)}, u32[]{:S(2)}, u32[]{:S(2)}) collective-permute-start(bf16[768,128]{1,0:T(8,128)(2,1)S(1)} %merge.5), channel_id=1, source_target_pairs={{0,2},{1,3},{2,0},{3,1},{4,6},{5,7},{6,4},{7,5},{8,10},{9,11},{10,... | collective-permute-start | bytes 589832 | tf_op jit(solution)/shard_map/ppermute | solution.py:50
  13.3 1.5 %collective-permute-start.3 = (bf16[768,128]{1,0:T(8,128)(2,1)S(1)}, bf16[768,128]{1,0:T(8,128)(2,1)S(1)}, u32[]{:S(2)}, u32[]{:S(2)}) collective-permute-start(bf16[768,128]{1,0:T(8,128)(2,1)S(1)} %merge.4), channel_id=1, source_target_pairs={{0,4},{1,5},{2,6},{3,7},{4,0},{5,1},{6,2},{7,3},{8,12},{9,13},{10,... | collective-permute-start | bytes 589832 | tf_op jit(solution)/shard_map/ppermute | solution.py:50
  14.7 1.1 %collective-permute-start.5 = (bf16[512,128]{1,0:T(8,128)(2,1)S(1)}, bf16[512,128]{1,0:T(8,128)(2,1)S(1)}, u32[]{:S(2)}, u32[]{:S(2)}) collective-permute-start(bf16[512,128]{1,0:T(8,128)(2,1)S(1)} %collective-permute-done.2.refs_1_.rest_5_.refs_3_), channel_id=1, source_target_pairs={{0,6},{1,7},{2,4},{3,5},{4,2},{5,3},{6,0},{7,1},{8,14},{9,15},{10,... | collective-permute-start | bytes 393224 | tf_op jit(solution)/shard_map/ppermute | solution.py:50
  15.8 0.1 collective-permute-start.6
  15.9 3.2 %second_half.1.k_ref = f32[3,128,128]{2,1,0:T(8,128)S(1)} custom-call(f32[3,64,128]{2,1,0:T(8,128)S(1)} %first_half.1.first_ref, s32[2]{0:T(128)} %len_hbm.1), custom_call_target="tpu_custom_call" | custom-call | flops 128 | bytes 128 | tf_op jit(solution)/shard_map/second_half/pallas_call | solution.py:215
  19.1 2.5 %project.1 = (f32[2,256,128]{2,1,0:T(8,128)S(1)}, bf16[2,256,4096]{2,1,0:T(8,128)(2,1)S(1)}) custom-call(s32[1]{0:T(128)} %bitcast.me_ref, bf16[256,4096]{1,0:T(8,128)(2,1)} %bitcast.3, bf16[256,4096]{1,0:T(8,128)(2,1)} %bitcast.4, bf16[512,128]{1,0:T(8,128)(2,1)S(1)} %pack.1.rest_2_.refs_0_, ...), custom_call_target="tpu_custom_call" | custom-call | flops 128 | bytes 128 | tf_op jit(solution)/shard_map/project/pallas_call | solution.py:318
  21.6 0.5 collective-permute-done.5.refs_2_.rest_5_
  22.1 0.0 collective-permute-done.4.refs_1_.rest_4_
  22.1 0.0 collective-permute-done.3.refs_0_.rest_3_
  22.1 0.1 collective-permute-start.7
  22.3 0.0 collective-permute-done.6.rest_1_
  22.3 1.9 %collective-permute-done.7.rest_2_ = bf16[2048,128]{1,0:T(8,128)(2,1)S(1)} collective-permute-done((bf16[2048,128]{1,0:T(8,128)(2,1)S(1)}, bf16[2048,128]{1,0:T(8,128)(2,1)S(1)}, u32[]{:S(2)}, u32[]{:S(2)}) %collective-permute-start.7) | collective-permute-done | bytes 524320 | tf_op jit(solution)/shard_map/ppermute | solution.py:50
  24.1 0.0 copy-start
  24.1 0.0 copy-start.1
  24.1 1.8 %whiten.1 = bf16[16,16,128]{2,1,0:T(8,128)(2,1)S(1)} custom-call(s32[1]{0:T(128)} %bitcast.me_ref, f32[2,256,128]{2,1,0:T(8,128)S(1)} %get-tuple-element.23.total_ref, f32[3,128,128]{2,1,0:T(8,128)S(1)} %second_half.1.k_ref, bf16[2,256,4096]{2,1,0:T(8,128)(2,1)S(1)} %get-tuple-element.25.rest_0_, bf16[2048,128]{1,0:T(8,128)(2,1)S(1)} %collective-permute-done.6.rest_1_, ...), custom_call_target="tpu_custom_call" | custom-call | flops 134217728 | bytes 4194304 | tf_op jit(solution)/shard_map/whiten/pallas_call | solution.py:367
  25.9 9.8 %all_to_all.10.white_ref = bf16[16,16,128]{2,1,0:T(8,128)(2,1)S(1)} all-to-all(bf16[16,16,128]{2,1,0:T(8,128)(2,1)S(1)} %whiten.1), channel_id=1, replica_groups={{11,9,7,5,15,13,3,1,10,8,6,4,14,12,2,0},{27,25,23,21,31,29,19,17,26,24,..., dimensions={0} | all-to-all | bytes 131072 | tf_op jit(solution)/shard_map/all_to_all | solution.py:381
  35.7 0.0 copy-done
  35.7 0.0 copy-done.1
  35.7 1.7 %score.1 = bf16[16,32,128]{2,1,0:T(8,128)(2,1)S(1)} custom-call(s32[1]{0:T(128)} %bitcast.me_ref, s32[2]{0:T(128)S(1)} %copy-done.1, bf16[16,16,128]{2,1,0:T(8,128)(2,1)S(1)} %all_to_all.10.white_ref, bf16[1536,1024]{1,0:T(8,128)(2,1)S(1)} %copy-done), custom_call_target="tpu_custom_call" | custom-call | flops 100663296 | bytes 3145728 | tf_op jit(solution)/shard_map/score/pallas_call | solution.py:413
  37.4 9.4 %all_to_all.11.a = bf16[16,32,128]{2,1,0:T(8,128)(2,1)S(1)} all-to-all(bf16[16,32,128]{2,1,0:T(8,128)(2,1)S(1)} %score.1), channel_id=1, replica_groups={{11,9,7,5,15,13,3,1,10,8,6,4,14,12,2,0},{27,25,23,21,31,29,19,17,26,24,..., dimensions={0} | all-to-all | bytes 262144 | tf_op jit(solution)/shard_map/all_to_all | solution.py:381
  46.7 0.9 %place.1 = bf16[32,96]{1,0:T(8,128)(2,1)} custom-call(bf16[16,32,128]{2,1,0:T(8,128)(2,1)S(1)} %all_to_all.11.a), custom_call_target="tpu_custom_call" | custom-call | tf_op jit(solution)/shard_map/place/pallas_call | solution.py:439
  (4 shorter events, 0.1 us)
Async XLA Ops:
  0.9 11.2 %collective-permute-start.2 = (bf16[512,128]{1,0:T(8,128)(2,1)S(1)}, bf16[512,128]{1,0:T(8,128)(2,1)S(1)}, u32[]{:S(2)}, u32[]{:S(2)}) collective-permute-start(bf16[512,128]{1,0:T(8,128)(2,1)S(1)} %pack.1.rest_2_.refs_0_), channel_id=1, source_target_pairs={{0,8},{1,9},{2,10},{3,11},{4,12},{5,13},{6,14},{7,15},{8,0},{9,1},... | collective-permute-start | bytes 393224 | tf_op jit(solution)/shard_map/ppermute | solution.py:50
  5.0 7.1 %collective-permute-start.1 = (bf16[512,128]{1,0:T(8,128)(2,1)S(1)}, bf16[512,128]{1,0:T(8,128)(2,1)S(1)}, u32[]{:S(2)}, u32[]{:S(2)}) collective-permute-start(bf16[512,128]{1,0:T(8,128)(2,1)S(1)} %pack.1.rest_2_.refs_0_), channel_id=1, source_target_pairs={{0,4},{1,5},{2,6},{3,7},{4,0},{5,1},{6,2},{7,3},{8,12},{9,13},{10,... | collective-permute-start | bytes 393224 | tf_op jit(solution)/shard_map/ppermute | solution.py:50
  6.6 5.6 %collective-permute-start = (bf16[512,128]{1,0:T(8,128)(2,1)S(1)}, bf16[512,128]{1,0:T(8,128)(2,1)S(1)}, u32[]{:S(2)}, u32[]{:S(2)}) collective-permute-start(bf16[512,128]{1,0:T(8,128)(2,1)S(1)} %pack.1.rest_2_.refs_0_), channel_id=1, source_target_pairs={{0,2},{1,3},{2,0},{3,1},{4,6},{5,7},{6,4},{7,5},{8,10},{9,11},{10,... | collective-permute-start | bytes 393224 | tf_op jit(solution)/shard_map/ppermute | solution.py:50
  12.2 9.9 %collective-permute-start.4 = (bf16[768,128]{1,0:T(8,128)(2,1)S(1)}, bf16[768,128]{1,0:T(8,128)(2,1)S(1)}, u32[]{:S(2)}, u32[]{:S(2)}) collective-permute-start(bf16[768,128]{1,0:T(8,128)(2,1)S(1)} %merge.5), channel_id=1, source_target_pairs={{0,2},{1,3},{2,0},{3,1},{4,6},{5,7},{6,4},{7,5},{8,10},{9,11},{10,... | collective-permute-start | bytes 589832 | tf_op jit(solution)/shard_map/ppermute | solution.py:50
  13.3 8.9 %collective-permute-start.3 = (bf16[768,128]{1,0:T(8,128)(2,1)S(1)}, bf16[768,128]{1,0:T(8,128)(2,1)S(1)}, u32[]{:S(2)}, u32[]{:S(2)}) collective-permute-start(bf16[768,128]{1,0:T(8,128)(2,1)S(1)} %merge.4), channel_id=1, source_target_pairs={{0,4},{1,5},{2,6},{3,7},{4,0},{5,1},{6,2},{7,3},{8,12},{9,13},{10,... | collective-permute-start | bytes 589832 | tf_op jit(solution)/shard_map/ppermute | solution.py:50
  14.7 7.4 %collective-permute-start.5 = (bf16[512,128]{1,0:T(8,128)(2,1)S(1)}, bf16[512,128]{1,0:T(8,128)(2,1)S(1)}, u32[]{:S(2)}, u32[]{:S(2)}) collective-permute-start(bf16[512,128]{1,0:T(8,128)(2,1)S(1)} %collective-permute-done.2.refs_1_.rest_5_.refs_3_), channel_id=1, source_target_pairs={{0,6},{1,7},{2,4},{3,5},{4,2},{5,3},{6,0},{7,1},{8,14},{9,15},{10,... | collective-permute-start | bytes 393224 | tf_op jit(solution)/shard_map/ppermute | solution.py:50
  15.8 6.4 %collective-permute-start.6 = (bf16[2048,128]{1,0:T(8,128)(2,1)S(1)}, bf16[2048,128]{1,0:T(8,128)(2,1)S(1)}, u32[]{:S(2)}, u32[]{:S(2)}) collective-permute-start(bf16[2048,128]{1,0:T(8,128)(2,1)S(1)} %merge.6), channel_id=1, source_target_pairs={{0,1},{1,0},{2,3},{3,2},{4,5},{5,4},{6,7},{7,6},{8,9},{9,8},{10,11... | collective-permute-start | bytes 1572872 | tf_op jit(solution)/shard_map/ppermute | solution.py:50
  22.1 2.0 %collective-permute-start.7 = (bf16[2048,128]{1,0:T(8,128)(2,1)S(1)}, bf16[2048,128]{1,0:T(8,128)(2,1)S(1)}, u32[]{:S(2)}, u32[]{:S(2)}) collective-permute-start(bf16[2048,128]{1,0:T(8,128)(2,1)S(1)} %merge.7), channel_id=1, source_target_pairs={{0,1},{1,0},{2,3},{3,2},{4,5},{5,4},{6,7},{7,6},{8,9},{9,8},{10,11... | collective-permute-start | bytes 1572872 | tf_op jit(solution)/shard_map/ppermute | solution.py:50
  24.1 11.6 %copy-start = (bf16[1536,1024]{1,0:T(8,128)(2,1)S(1)}, bf16[1536,1024]{1,0:T(8,128)(2,1)}, u32[]{:S(2)}) copy-start(bf16[1536,1024]{1,0:T(8,128)(2,1)} %bank_ref.1) | copy-start | bytes 9437188
  24.1 11.6 %copy-start.1 = (s32[2]{0:T(128)S(1)}, s32[2]{0:T(128)}, u32[]{:S(2)}) copy-start(s32[2]{0:T(128)} %ids_ref.1) | copy-start | bytes 28

commit v2 on v1

--- a/solution.py
+++ b/solution.py
@@ -397,8 +397,8 @@
     for s in range(seqs):
         tail = jnp.where(row == place * seqs + s, ids_ref[s].astype(jnp.float32), tail)
     partial = lax.dot_general(
-        columns, bank_ref[...], (((1,), (1,)), ((), ())), preferred_element_type=jnp.float32
-    )
+        bank_ref[...], columns, (((1,), (1,)), ((), ())), preferred_element_type=jnp.float32
+    ).T
     for d in range(n):
         at = exchange_order(n).index(d)
         out_ref[at, :, :queries] = partial[:, d * queries : (d + 1) * queries].astype(out_ref.dtype)

time: 47.9 us -> 48 us (level)
  no operation moved by 1% of the time
where the time goes in v2:
time: 48 us; the launch traced here: 47.7 us
  blocking collectives  19.1 us (40%)
  Pallas kernels  15.2 us (32%)
  starting transfers between devices  11 us (23%)
  waiting for transfers between devices  2.33 us (5%)
    all_to_all x2, blocking collectives, exchanged(): lax.all_to_all(value, 'coord', split_axis=0, concat_axis=0, axis_index_gr...  19.1 us
    ppermute x8, starting transfers between devices, moved(): return lax.ppermute(value, 'coord', pairs)  11 us
    pallas_call x1, Pallas kernels, first_half(): pl.pallas_call(first_half_kernel, out_shape=jax.ShapeDtypeStruct((3, size...  4.03 us
    pallas_call x1, Pallas kernels, second_half(): pl.pallas_call(second_half_kernel, out_shape=jax.ShapeDtypeStruct((3, siz...  3.19 us
    pallas_call x1, Pallas kernels, project(): pl.pallas_call(functools.partial(project_kernel, n, early, seqs), out_sha...  2.51 us
    ppermute x8, waiting for transfers between devices, moved(): return lax.ppermute(value, 'coord', pairs)  2.33 us
    pallas_call x1, Pallas kernels, whitened_blocks(): pl.pallas_call(functools.partial(whiten_kernel, n, seqs, late), out_shape...  1.8 us
    pallas_call x1, Pallas kernels, partial_scores(): pl.pallas_call(functools.partial(score_kernel, n), out_shape=jax.ShapeDty...  1.79 us
  transfers between devices with their start and end apart: 8, of which 2 were waited for; matrix products, arithmetic and copies ran while one was open for 0% of the time, Pallas kernels for 21%

profile of v2, /device:TPU:0, one launch (start us, length us, event | category | flops | bytes accessed | tf_op | source)
XLA Modules:
  0.0 47.7 jit_solution(18123697070807046124)
XLA Ops:
  0.0 0.9 %pack.1.rest_2_.refs_0_ = bf16[512,128]{1,0:T(8,128)(2,1)S(1)} custom-call(bf16[256,128]{1,0:T(8,128)(2,1)} %first_hbm.1, bf16[256,128]{1,0:T(8,128)(2,1)} %second_hbm.1), custom_call_target="tpu_custom_call" | custom-call | tf_op jit(solution)/shard_map/pack/pallas_call | solution.py:79
  0.9 4.1 %collective-permute-start.2 = (bf16[512,128]{1,0:T(8,128)(2,1)S(1)}, bf16[512,128]{1,0:T(8,128)(2,1)S(1)}, u32[]{:S(2)}, u32[]{:S(2)}) collective-permute-start(bf16[512,128]{1,0:T(8,128)(2,1)S(1)} %pack.1.rest_2_.refs_0_), channel_id=1, source_target_pairs={{0,8},{1,9},{2,10},{3,11},{4,12},{5,13},{6,14},{7,15},{8,0},{9,1},... | collective-permute-start | bytes 393224 | tf_op jit(solution)/shard_map/ppermute | solution.py:50
  5.0 1.6 %collective-permute-start.1 = (bf16[512,128]{1,0:T(8,128)(2,1)S(1)}, bf16[512,128]{1,0:T(8,128)(2,1)S(1)}, u32[]{:S(2)}, u32[]{:S(2)}) collective-permute-start(bf16[512,128]{1,0:T(8,128)(2,1)S(1)} %pack.1.rest_2_.refs_0_), channel_id=1, source_target_pairs={{0,4},{1,5},{2,6},{3,7},{4,0},{5,1},{6,2},{7,3},{8,12},{9,13},{10,... | collective-permute-start | bytes 393224 | tf_op jit(solution)/shard_map/ppermute | solution.py:50
  6.6 1.5 %collective-permute-start = (bf16[512,128]{1,0:T(8,128)(2,1)S(1)}, bf16[512,128]{1,0:T(8,128)(2,1)S(1)}, u32[]{:S(2)}, u32[]{:S(2)}) collective-permute-start(bf16[512,128]{1,0:T(8,128)(2,1)S(1)} %pack.1.rest_2_.refs_0_), channel_id=1, source_target_pairs={{0,2},{1,3},{2,0},{3,1},{4,6},{5,7},{6,4},{7,5},{8,10},{9,11},{10,... | collective-permute-start | bytes 393224 | tf_op jit(solution)/shard_map/ppermute | solution.py:50
  8.1 4.0 %first_half.1.first_ref = f32[3,64,128]{2,1,0:T(8,128)S(1)} custom-call(f32[128,128]{1,0:T(8,128)} %cov_in_hbm.1, f32[128,128]{1,0:T(8,128)} %cov_out_hbm.1), custom_call_target="tpu_custom_call" | custom-call | flops 128 | bytes 128 | tf_op jit(solution)/shard_map/first_half/pallas_call | solution.py:201
  12.1 0.0 collective-permute-done.2.refs_1_.rest_5_.refs_3_
  12.1 0.0 collective-permute-done.1.refs_0_.rest_4_.refs_2_
  12.1 0.0 collective-permute-done.refs_0_.rest_3_.refs_1_
  12.2 1.1 %collective-permute-start.4 = (bf16[768,128]{1,0:T(8,128)(2,1)S(1)}, bf16[768,128]{1,0:T(8,128)(2,1)S(1)}, u32[]{:S(2)}, u32[]{:S(2)}) collective-permute-start(bf16[768,128]{1,0:T(8,128)(2,1)S(1)} %merge.5), channel_id=1, source_target_pairs={{0,2},{1,3},{2,0},{3,1},{4,6},{5,7},{6,4},{7,5},{8,10},{9,11},{10,... | collective-permute-start | bytes 589832 | tf_op jit(solution)/shard_map/ppermute | solution.py:50
  13.3 1.5 %collective-permute-start.3 = (bf16[768,128]{1,0:T(8,128)(2,1)S(1)}, bf16[768,128]{1,0:T(8,128)(2,1)S(1)}, u32[]{:S(2)}, u32[]{:S(2)}) collective-permute-start(bf16[768,128]{1,0:T(8,128)(2,1)S(1)} %merge.4), channel_id=1, source_target_pairs={{0,4},{1,5},{2,6},{3,7},{4,0},{5,1},{6,2},{7,3},{8,12},{9,13},{10,... | collective-permute-start | bytes 589832 | tf_op jit(solution)/shard_map/ppermute | solution.py:50
  14.7 1.1 %collective-permute-start.5 = (bf16[512,128]{1,0:T(8,128)(2,1)S(1)}, bf16[512,128]{1,0:T(8,128)(2,1)S(1)}, u32[]{:S(2)}, u32[]{:S(2)}) collective-permute-start(bf16[512,128]{1,0:T(8,128)(2,1)S(1)} %collective-permute-done.2.refs_1_.rest_5_.refs_3_), channel_id=1, source_target_pairs={{0,6},{1,7},{2,4},{3,5},{4,2},{5,3},{6,0},{7,1},{8,14},{9,15},{10,... | collective-permute-start | bytes 393224 | tf_op jit(solution)/shard_map/ppermute | solution.py:50
  15.8 0.1 collective-permute-start.6
  15.9 3.2 %second_half.1.k_ref = f32[3,128,128]{2,1,0:T(8,128)S(1)} custom-call(f32[3,64,128]{2,1,0:T(8,128)S(1)} %first_half.1.first_ref, s32[2]{0:T(128)} %len_hbm.1), custom_call_target="tpu_custom_call" | custom-call | flops 128 | bytes 128 | tf_op jit(solution)/shard_map/second_half/pallas_call | solution.py:215
  19.1 2.5 %project.1 = (f32[2,256,128]{2,1,0:T(8,128)S(1)}, bf16[2,256,4096]{2,1,0:T(8,128)(2,1)S(1)}) custom-call(s32[1]{0:T(128)} %bitcast.me_ref, bf16[256,4096]{1,0:T(8,128)(2,1)} %bitcast.3, bf16[256,4096]{1,0:T(8,128)(2,1)} %bitcast.4, bf16[512,128]{1,0:T(8,128)(2,1)S(1)} %pack.1.rest_2_.refs_0_, ...), custom_call_target="tpu_custom_call" | custom-call | flops 128 | bytes 128 | tf_op jit(solution)/shard_map/project/pallas_call | solution.py:318
  21.6 0.5 collective-permute-done.5.refs_2_.rest_5_
  22.1 0.0 collective-permute-done.4.refs_1_.rest_4_
  22.1 0.0 collective-permute-done.3.refs_0_.rest_3_
  22.1 0.1 collective-permute-start.7
  22.3 0.0 collective-permute-done.6.rest_1_
  22.3 1.9 %collective-permute-done.7.rest_2_ = bf16[2048,128]{1,0:T(8,128)(2,1)S(1)} collective-permute-done((bf16[2048,128]{1,0:T(8,128)(2,1)S(1)}, bf16[2048,128]{1,0:T(8,128)(2,1)S(1)}, u32[]{:S(2)}, u32[]{:S(2)}) %collective-permute-start.7) | collective-permute-done | bytes 524320 | tf_op jit(solution)/shard_map/ppermute | solution.py:50
  24.1 0.0 copy-start
  24.1 0.0 copy-start.1
  24.1 1.8 %whiten.1 = bf16[16,16,128]{2,1,0:T(8,128)(2,1)S(1)} custom-call(s32[1]{0:T(128)} %bitcast.me_ref, f32[2,256,128]{2,1,0:T(8,128)S(1)} %get-tuple-element.23.total_ref, f32[3,128,128]{2,1,0:T(8,128)S(1)} %second_half.1.k_ref, bf16[2,256,4096]{2,1,0:T(8,128)(2,1)S(1)} %get-tuple-element.25.rest_0_, bf16[2048,128]{1,0:T(8,128)(2,1)S(1)} %collective-permute-done.6.rest_1_, ...), custom_call_target="tpu_custom_call" | custom-call | flops 134217728 | bytes 4194304 | tf_op jit(solution)/shard_map/whiten/pallas_call | solution.py:367
  25.9 9.8 %all_to_all.10.white_ref = bf16[16,16,128]{2,1,0:T(8,128)(2,1)S(1)} all-to-all(bf16[16,16,128]{2,1,0:T(8,128)(2,1)S(1)} %whiten.1), channel_id=1, replica_groups={{11,9,7,5,15,13,3,1,10,8,6,4,14,12,2,0},{27,25,23,21,31,29,19,17,26,24,..., dimensions={0} | all-to-all | bytes 131072 | tf_op jit(solution)/shard_map/all_to_all | solution.py:381
  35.7 0.0 copy-done
  35.7 0.0 copy-done.1
  35.7 1.8 %score.1 = bf16[16,32,128]{2,1,0:T(8,128)(2,1)S(1)} custom-call(s32[1]{0:T(128)} %bitcast.me_ref, s32[2]{0:T(128)S(1)} %copy-done.1, bf16[16,16,128]{2,1,0:T(8,128)(2,1)S(1)} %all_to_all.10.white_ref, bf16[1536,1024]{1,0:T(8,128)(2,1)S(1)} %copy-done), custom_call_target="tpu_custom_call" | custom-call | flops 100663296 | bytes 3145728 | tf_op jit(solution)/shard_map/score/pallas_call | solution.py:413
  37.5 9.4 %all_to_all.11.a = bf16[16,32,128]{2,1,0:T(8,128)(2,1)S(1)} all-to-all(bf16[16,32,128]{2,1,0:T(8,128)(2,1)S(1)} %score.1), channel_id=1, replica_groups={{11,9,7,5,15,13,3,1,10,8,6,4,14,12,2,0},{27,25,23,21,31,29,19,17,26,24,..., dimensions={0} | all-to-all | bytes 262144 | tf_op jit(solution)/shard_map/all_to_all | solution.py:381
  46.9 0.9 %place.1 = bf16[32,96]{1,0:T(8,128)(2,1)} custom-call(bf16[16,32,128]{2,1,0:T(8,128)(2,1)S(1)} %all_to_all.11.a), custom_call_target="tpu_custom_call" | custom-call | tf_op jit(solution)/shard_map/place/pallas_call | solution.py:439
  (4 shorter events, 0.1 us)
Async XLA Ops:
  0.9 11.2 %collective-permute-start.2 = (bf16[512,128]{1,0:T(8,128)(2,1)S(1)}, bf16[512,128]{1,0:T(8,128)(2,1)S(1)}, u32[]{:S(2)}, u32[]{:S(2)}) collective-permute-start(bf16[512,128]{1,0:T(8,128)(2,1)S(1)} %pack.1.rest_2_.refs_0_), channel_id=1, source_target_pairs={{0,8},{1,9},{2,10},{3,11},{4,12},{5,13},{6,14},{7,15},{8,0},{9,1},... | collective-permute-start | bytes 393224 | tf_op jit(solution)/shard_map/ppermute | solution.py:50
  5.0 7.1 %collective-permute-start.1 = (bf16[512,128]{1,0:T(8,128)(2,1)S(1)}, bf16[512,128]{1,0:T(8,128)(2,1)S(1)}, u32[]{:S(2)}, u32[]{:S(2)}) collective-permute-start(bf16[512,128]{1,0:T(8,128)(2,1)S(1)} %pack.1.rest_2_.refs_0_), channel_id=1, source_target_pairs={{0,4},{1,5},{2,6},{3,7},{4,0},{5,1},{6,2},{7,3},{8,12},{9,13},{10,... | collective-permute-start | bytes 393224 | tf_op jit(solution)/shard_map/ppermute | solution.py:50
  6.6 5.6 %collective-permute-start = (bf16[512,128]{1,0:T(8,128)(2,1)S(1)}, bf16[512,128]{1,0:T(8,128)(2,1)S(1)}, u32[]{:S(2)}, u32[]{:S(2)}) collective-permute-start(bf16[512,128]{1,0:T(8,128)(2,1)S(1)} %pack.1.rest_2_.refs_0_), channel_id=1, source_target_pairs={{0,2},{1,3},{2,0},{3,1},{4,6},{5,7},{6,4},{7,5},{8,10},{9,11},{10,... | collective-permute-start | bytes 393224 | tf_op jit(solution)/shard_map/ppermute | solution.py:50
  12.2 9.9 %collective-permute-start.4 = (bf16[768,128]{1,0:T(8,128)(2,1)S(1)}, bf16[768,128]{1,0:T(8,128)(2,1)S(1)}, u32[]{:S(2)}, u32[]{:S(2)}) collective-permute-start(bf16[768,128]{1,0:T(8,128)(2,1)S(1)} %merge.5), channel_id=1, source_target_pairs={{0,2},{1,3},{2,0},{3,1},{4,6},{5,7},{6,4},{7,5},{8,10},{9,11},{10,... | collective-permute-start | bytes 589832 | tf_op jit(solution)/shard_map/ppermute | solution.py:50
  13.3 8.9 %collective-permute-start.3 = (bf16[768,128]{1,0:T(8,128)(2,1)S(1)}, bf16[768,128]{1,0:T(8,128)(2,1)S(1)}, u32[]{:S(2)}, u32[]{:S(2)}) collective-permute-start(bf16[768,128]{1,0:T(8,128)(2,1)S(1)} %merge.4), channel_id=1, source_target_pairs={{0,4},{1,5},{2,6},{3,7},{4,0},{5,1},{6,2},{7,3},{8,12},{9,13},{10,... | collective-permute-start | bytes 589832 | tf_op jit(solution)/shard_map/ppermute | solution.py:50
  14.7 7.4 %collective-permute-start.5 = (bf16[512,128]{1,0:T(8,128)(2,1)S(1)}, bf16[512,128]{1,0:T(8,128)(2,1)S(1)}, u32[]{:S(2)}, u32[]{:S(2)}) collective-permute-start(bf16[512,128]{1,0:T(8,128)(2,1)S(1)} %collective-permute-done.2.refs_1_.rest_5_.refs_3_), channel_id=1, source_target_pairs={{0,6},{1,7},{2,4},{3,5},{4,2},{5,3},{6,0},{7,1},{8,14},{9,15},{10,... | collective-permute-start | bytes 393224 | tf_op jit(solution)/shard_map/ppermute | solution.py:50
  15.8 6.4 %collective-permute-start.6 = (bf16[2048,128]{1,0:T(8,128)(2,1)S(1)}, bf16[2048,128]{1,0:T(8,128)(2,1)S(1)}, u32[]{:S(2)}, u32[]{:S(2)}) collective-permute-start(bf16[2048,128]{1,0:T(8,128)(2,1)S(1)} %merge.6), channel_id=1, source_target_pairs={{0,1},{1,0},{2,3},{3,2},{4,5},{5,4},{6,7},{7,6},{8,9},{9,8},{10,11... | collective-permute-start | bytes 1572872 | tf_op jit(solution)/shard_map/ppermute | solution.py:50
  22.1 2.0 %collective-permute-start.7 = (bf16[2048,128]{1,0:T(8,128)(2,1)S(1)}, bf16[2048,128]{1,0:T(8,128)(2,1)S(1)}, u32[]{:S(2)}, u32[]{:S(2)}) collective-permute-start(bf16[2048,128]{1,0:T(8,128)(2,1)S(1)} %merge.7), channel_id=1, source_target_pairs={{0,1},{1,0},{2,3},{3,2},{4,5},{5,4},{6,7},{7,6},{8,9},{9,8},{10,11... | collective-permute-start | bytes 1572872 | tf_op jit(solution)/shard_map/ppermute | solution.py:50
  24.1 11.6 %copy-start = (bf16[1536,1024]{1,0:T(8,128)(2,1)S(1)}, bf16[1536,1024]{1,0:T(8,128)(2,1)}, u32[]{:S(2)}) copy-start(bf16[1536,1024]{1,0:T(8,128)(2,1)} %bank_ref.1) | copy-start | bytes 9437188
  24.1 11.6 %copy-start.1 = (s32[2]{0:T(128)S(1)}, s32[2]{0:T(128)}, u32[]{:S(2)}) copy-start(s32[2]{0:T(128)} %ids_ref.1) | copy-start | bytes 28

commit v3 on v1

--- a/solution.py
+++ b/solution.py
@@ -328,18 +328,42 @@
     )(me, pinned(activations), pinned(out_grads), *blocks)
 
 
+def add_products(n, late, me_ref, held, blocks, sums):
+    source = sources(me_ref[0], n)
+    rows = held.shape[2] // n
+    for which, t, operand, at in late:
+        columns = pl.ds(pl.multiple_of(source[which] * rows, rows), rows)
+        block = blocks[operand][at : at + rows, :]
+        sums[t] = sums[t] + jnp.dot(held[t, :, columns], block, preferred_element_type=jnp.float32)
+
+
+def extend_kernel(n, late, me_ref, total_ref, held, *rest):
+    blocks, out_ref = rest[:-1], rest[-1]
+    sums = [total_ref[0], total_ref[1]]
+    add_products(n, late, me_ref, held, blocks, sums)
+    out_ref[0] = sums[0]
+    out_ref[1] = sums[1]
+
+
+def extended(me, total, inputs, late, blocks, n):
+    return pl.pallas_call(
+        functools.partial(extend_kernel, n, late),
+        out_shape=jax.ShapeDtypeStruct(total.shape, total.dtype),
+        in_specs=[SMEM] + [VMEM] * (2 + len(blocks)),
+        out_specs=VMEM,
+        compiler_params=pltpu.CompilerParams(vmem_limit_bytes=16 << 20),
+        cost_estimate=pl.CostEstimate(flops=total.size, bytes_accessed=total.size, transcendentals=0),
+        name="extend",
+    )(me, total, inputs, *blocks)
+
+
 def whiten_kernel(n, seqs, late, me_ref, total_ref, k_ref, *rest):
     operands, (out_ref, white) = rest[:-2], rest[-2:]
     rank = k_ref.shape[1]
     sums = [total_ref[0], total_ref[1]]
     if late:
         held, *blocks = operands
-        source = sources(me_ref[0], n)
-        rows = held.shape[2] // n
-        for which, t, operand, at in late:
-            columns = pl.ds(pl.multiple_of(source[which] * rows, rows), rows)
-            block = blocks[operand][at : at + rows, :]
-            sums[t] = sums[t] + jnp.dot(held[t, :, columns], block, preferred_element_type=jnp.float32)
+        add_products(n, late, me_ref, held, blocks, sums)
     length = total_ref.shape[1] // seqs
     share = rank // n
     grads = []
@@ -498,16 +522,16 @@
         across = [moved(merge([(held[at], 0, 2 * rows) for at in early]), (0, 0, 1), n)]
         waiting, total, k = lax.optimization_barrier(([arrived for arrived, _ in arrivals], total, k))
         across.append(moved(merge([(arrived, 0, arrived.shape[0]) for arrived in waiting]), (0, 0, 1), n))
-        operands = [inputs, *across, *waiting]
-        late = [
-            (order.index(at), t, 2 + i, j * rows)
+        operands = [inputs, across[1]]
+        sooner = [
+            (order.index(at), t, 1 + i, j * rows)
             for i, (_, group) in enumerate(arrivals)
             for j, (at, t) in enumerate(group)
         ]
         crossed = [[(at, t) for at in early for t in range(2)], [to for _, group in arrivals for to in group]]
-        late += [
-            (order.index((*at[:2], 1)), t, i, j * rows) for i, part in enumerate(crossed) for j, (at, t) in enumerate(part)
-        ]
+        sooner += [(order.index((*at[:2], 1)), t, 0, j * rows) for j, (at, t) in enumerate(crossed[0])]
+        late = [(order.index((*at[:2], 1)), t, 0, j * rows) for j, (at, t) in enumerate(crossed[1])]
+        total = extended(me, total, inputs, sooner, [across[0], *waiting], n)
     else:
         for at in order:
             if at[2] == 0:

time: 47.9 us -> 47.3 us (0.987)
  waiting for transfers between devices: 2.33 us -> 1.59 us
    ppermute x8, waiting for transfers between devices: 2.33 us -> 1.59 us  [moved(): return lax.ppermute(value, 'coord', pairs)]
    pallas_call x0 -> x1, Pallas kernels: none -> 0.71 us  [extended(): pl.pallas_call(functools.partial(extend_kernel, n, late), out_shape=jax.S...]
    pallas_call x1, Pallas kernels: 1.8 us -> 1.23 us  [whitened_blocks(): pl.pallas_call(functools.partial(whiten_kernel, n, seqs, late), out_shape...]
  transfers between devices with their start and end apart: 8 -> 8, of which waited for: 2 -> 2; matrix products, arithmetic and copies ran while one was open for 0% -> 0% of each run, Pallas kernels for 21% -> 22%
where the time goes in v3:
time: 47.3 us; the launch traced here: 47 us
  blocking collectives  19.1 us (40%)
  Pallas kernels  15.2 us (32%)
  starting transfers between devices  11 us (23%)
  waiting for transfers between devices  1.59 us (3%)
    all_to_all x2, blocking collectives, exchanged(): lax.all_to_all(value, 'coord', split_axis=0, concat_axis=0, axis_index_gr...  19.1 us
    ppermute x8, starting transfers between devices, moved(): return lax.ppermute(value, 'coord', pairs)  11 us
    pallas_call x1, Pallas kernels, first_half(): pl.pallas_call(first_half_kernel, out_shape=jax.ShapeDtypeStruct((3, size...  4.03 us
    pallas_call x1, Pallas kernels, second_half(): pl.pallas_call(second_half_kernel, out_shape=jax.ShapeDtypeStruct((3, siz...  3.19 us
    pallas_call x1, Pallas kernels, project(): pl.pallas_call(functools.partial(project_kernel, n, early, seqs), out_sha...  2.51 us
    pallas_call x1, Pallas kernels, partial_scores(): pl.pallas_call(functools.partial(score_kernel, n), out_shape=jax.ShapeDty...  1.66 us
    ppermute x8, waiting for transfers between devices, moved(): return lax.ppermute(value, 'coord', pairs)  1.59 us
    pallas_call x1, Pallas kernels, whitened_blocks(): pl.pallas_call(functools.partial(whiten_kernel, n, seqs, late), out_shape...  1.23 us
  transfers between devices with their start and end apart: 8, of which 2 were waited for; matrix products, arithmetic and copies ran while one was open for 0% of the time, Pallas kernels for 22%

profile of v3, /device:TPU:0, one launch (start us, length us, event | category | flops | bytes accessed | tf_op | source)
XLA Modules:
  0.0 47.0 jit_solution(14969763292173938972)
XLA Ops:
  0.0 0.9 %pack.1.rest_2_.refs_0_ = bf16[512,128]{1,0:T(8,128)(2,1)S(1)} custom-call(bf16[256,128]{1,0:T(8,128)(2,1)} %first_hbm.1, bf16[256,128]{1,0:T(8,128)(2,1)} %second_hbm.1), custom_call_target="tpu_custom_call" | custom-call | tf_op jit(solution)/shard_map/pack/pallas_call | solution.py:79
  0.9 4.1 %collective-permute-start.2 = (bf16[512,128]{1,0:T(8,128)(2,1)S(1)}, bf16[512,128]{1,0:T(8,128)(2,1)S(1)}, u32[]{:S(2)}, u32[]{:S(2)}) collective-permute-start(bf16[512,128]{1,0:T(8,128)(2,1)S(1)} %pack.1.rest_2_.refs_0_), channel_id=1, source_target_pairs={{0,8},{1,9},{2,10},{3,11},{4,12},{5,13},{6,14},{7,15},{8,0},{9,1},... | collective-permute-start | bytes 393224 | tf_op jit(solution)/shard_map/ppermute | solution.py:50
  5.0 1.6 %collective-permute-start.1 = (bf16[512,128]{1,0:T(8,128)(2,1)S(1)}, bf16[512,128]{1,0:T(8,128)(2,1)S(1)}, u32[]{:S(2)}, u32[]{:S(2)}) collective-permute-start(bf16[512,128]{1,0:T(8,128)(2,1)S(1)} %pack.1.rest_2_.refs_0_), channel_id=1, source_target_pairs={{0,4},{1,5},{2,6},{3,7},{4,0},{5,1},{6,2},{7,3},{8,12},{9,13},{10,... | collective-permute-start | bytes 393224 | tf_op jit(solution)/shard_map/ppermute | solution.py:50
  6.6 1.5 %collective-permute-start = (bf16[512,128]{1,0:T(8,128)(2,1)S(1)}, bf16[512,128]{1,0:T(8,128)(2,1)S(1)}, u32[]{:S(2)}, u32[]{:S(2)}) collective-permute-start(bf16[512,128]{1,0:T(8,128)(2,1)S(1)} %pack.1.rest_2_.refs_0_), channel_id=1, source_target_pairs={{0,2},{1,3},{2,0},{3,1},{4,6},{5,7},{6,4},{7,5},{8,10},{9,11},{10,... | collective-permute-start | bytes 393224 | tf_op jit(solution)/shard_map/ppermute | solution.py:50
  8.1 4.0 %first_half.1.first_ref = f32[3,64,128]{2,1,0:T(8,128)S(1)} custom-call(f32[128,128]{1,0:T(8,128)} %cov_in_hbm.1, f32[128,128]{1,0:T(8,128)} %cov_out_hbm.1), custom_call_target="tpu_custom_call" | custom-call | flops 128 | bytes 128 | tf_op jit(solution)/shard_map/first_half/pallas_call | solution.py:201
  12.1 0.0 collective-permute-done.2.refs_1_.rest_5_.refs_3_
  12.1 0.0 collective-permute-done.1.refs_0_.rest_4_.refs_2_
  12.1 0.0 collective-permute-done.refs_0_.rest_3_.refs_1_
  12.2 1.1 %collective-permute-start.4 = (bf16[768,128]{1,0:T(8,128)(2,1)S(1)}, bf16[768,128]{1,0:T(8,128)(2,1)S(1)}, u32[]{:S(2)}, u32[]{:S(2)}) collective-permute-start(bf16[768,128]{1,0:T(8,128)(2,1)S(1)} %merge.5), channel_id=1, source_target_pairs={{0,2},{1,3},{2,0},{3,1},{4,6},{5,7},{6,4},{7,5},{8,10},{9,11},{10,... | collective-permute-start | bytes 589832 | tf_op jit(solution)/shard_map/ppermute | solution.py:50
  13.3 1.5 %collective-permute-start.3 = (bf16[768,128]{1,0:T(8,128)(2,1)S(1)}, bf16[768,128]{1,0:T(8,128)(2,1)S(1)}, u32[]{:S(2)}, u32[]{:S(2)}) collective-permute-start(bf16[768,128]{1,0:T(8,128)(2,1)S(1)} %merge.4), channel_id=1, source_target_pairs={{0,4},{1,5},{2,6},{3,7},{4,0},{5,1},{6,2},{7,3},{8,12},{9,13},{10,... | collective-permute-start | bytes 589832 | tf_op jit(solution)/shard_map/ppermute | solution.py:50
  14.7 1.1 %collective-permute-start.5 = (bf16[512,128]{1,0:T(8,128)(2,1)S(1)}, bf16[512,128]{1,0:T(8,128)(2,1)S(1)}, u32[]{:S(2)}, u32[]{:S(2)}) collective-permute-start(bf16[512,128]{1,0:T(8,128)(2,1)S(1)} %collective-permute-done.2.refs_1_.rest_5_.refs_3_), channel_id=1, source_target_pairs={{0,6},{1,7},{2,4},{3,5},{4,2},{5,3},{6,0},{7,1},{8,14},{9,15},{10,... | collective-permute-start | bytes 393224 | tf_op jit(solution)/shard_map/ppermute | solution.py:50
  15.8 0.1 collective-permute-start.6
  15.9 3.2 %second_half.1.k_ref = f32[3,128,128]{2,1,0:T(8,128)S(1)} custom-call(f32[3,64,128]{2,1,0:T(8,128)S(1)} %first_half.1.first_ref, s32[2]{0:T(128)} %len_hbm.1), custom_call_target="tpu_custom_call" | custom-call | flops 128 | bytes 128 | tf_op jit(solution)/shard_map/second_half/pallas_call | solution.py:215
  19.1 2.5 %project.1 = (f32[2,256,128]{2,1,0:T(8,128)S(1)}, bf16[2,256,4096]{2,1,0:T(8,128)(2,1)S(1)}) custom-call(s32[1]{0:T(128)} %bitcast.me_ref, bf16[256,4096]{1,0:T(8,128)(2,1)} %bitcast.3, bf16[256,4096]{1,0:T(8,128)(2,1)} %bitcast.4, bf16[512,128]{1,0:T(8,128)(2,1)S(1)} %pack.1.rest_2_.refs_0_, ...), custom_call_target="tpu_custom_call" | custom-call | flops 128 | bytes 128 | tf_op jit(solution)/shard_map/project/pallas_call | solution.py:318
  21.6 0.5 collective-permute-done.5.rest_3_.refs_2_
  22.1 0.0 collective-permute-done.4.rest_2_.refs_1_
  22.1 0.0 collective-permute-done.3.rest_1_.refs_0_
  22.1 0.1 collective-permute-start.7
  22.3 0.0 collective-permute-done.6.rest_0_
  22.3 0.7 %extend.1.total_ref = f32[2,256,128]{2,1,0:T(8,128)S(1)} custom-call(s32[1]{0:T(128)} %bitcast.me_ref, f32[2,256,128]{2,1,0:T(8,128)S(1)} %get-tuple-element.23.total_ref, bf16[2,256,4096]{2,1,0:T(8,128)(2,1)S(1)} %get-tuple-element.24.held.rest_0_, bf16[2048,128]{1,0:T(8,128)(2,1)S(1)} %collective-permute-done.6.rest_0_, ...), custom_call_target="tpu_custom_call" | custom-call | flops 65536 | bytes 65536 | tf_op jit(solution)/shard_map/extend/pallas_call | solution.py:349
  23.0 0.0 copy-start
  23.0 0.0 copy-start.1
  23.0 1.1 %collective-permute-done.7.rest_1_ = bf16[2048,128]{1,0:T(8,128)(2,1)S(1)} collective-permute-done((bf16[2048,128]{1,0:T(8,128)(2,1)S(1)}, bf16[2048,128]{1,0:T(8,128)(2,1)S(1)}, u32[]{:S(2)}, u32[]{:S(2)}) %collective-permute-start.7) | collective-permute-done | bytes 524320 | tf_op jit(solution)/shard_map/ppermute | solution.py:50
  24.1 1.2 %whiten.1 = bf16[16,16,128]{2,1,0:T(8,128)(2,1)S(1)} custom-call(s32[1]{0:T(128)} %bitcast.me_ref, f32[2,256,128]{2,1,0:T(8,128)S(1)} %extend.1.total_ref, f32[3,128,128]{2,1,0:T(8,128)S(1)} %second_half.1.k_ref, bf16[2,256,4096]{2,1,0:T(8,128)(2,1)S(1)} %get-tuple-element.24.held.rest_0_, bf16[2048,128]{1,0:T(8,128)(2,1)S(1)} %collective-permute-done.7.rest_1_), custom_call_target="tpu_custom_call" | custom-call | flops 134217728 | bytes 4194304 | tf_op jit(solution)/shard_map/whiten/pallas_call | solution.py:391
  25.4 9.8 %all_to_all.10.white_ref = bf16[16,16,128]{2,1,0:T(8,128)(2,1)S(1)} all-to-all(bf16[16,16,128]{2,1,0:T(8,128)(2,1)S(1)} %whiten.1), channel_id=1, replica_groups={{11,9,7,5,15,13,3,1,10,8,6,4,14,12,2,0},{27,25,23,21,31,29,19,17,26,24,..., dimensions={0} | all-to-all | bytes 131072 | tf_op jit(solution)/shard_map/all_to_all | solution.py:405
  35.1 0.0 copy-done
  35.1 0.0 copy-done.1
  35.1 1.7 %score.1 = bf16[16,32,128]{2,1,0:T(8,128)(2,1)S(1)} custom-call(s32[1]{0:T(128)} %bitcast.me_ref, s32[2]{0:T(128)S(1)} %copy-done.1, bf16[16,16,128]{2,1,0:T(8,128)(2,1)S(1)} %all_to_all.10.white_ref, bf16[1536,1024]{1,0:T(8,128)(2,1)S(1)} %copy-done), custom_call_target="tpu_custom_call" | custom-call | flops 100663296 | bytes 3145728 | tf_op jit(solution)/shard_map/score/pallas_call | solution.py:437
  36.8 9.4 %all_to_all.11.a = bf16[16,32,128]{2,1,0:T(8,128)(2,1)S(1)} all-to-all(bf16[16,32,128]{2,1,0:T(8,128)(2,1)S(1)} %score.1), channel_id=1, replica_groups={{11,9,7,5,15,13,3,1,10,8,6,4,14,12,2,0},{27,25,23,21,31,29,19,17,26,24,..., dimensions={0} | all-to-all | bytes 262144 | tf_op jit(solution)/shard_map/all_to_all | solution.py:405
  46.2 0.9 %place.1 = bf16[32,96]{1,0:T(8,128)(2,1)} custom-call(bf16[16,32,128]{2,1,0:T(8,128)(2,1)S(1)} %all_to_all.11.a), custom_call_target="tpu_custom_call" | custom-call | tf_op jit(solution)/shard_map/place/pallas_call | solution.py:463
  (4 shorter events, 0.1 us)
Async XLA Ops:
  0.9 11.2 %collective-permute-start.2 = (bf16[512,128]{1,0:T(8,128)(2,1)S(1)}, bf16[512,128]{1,0:T(8,128)(2,1)S(1)}, u32[]{:S(2)}, u32[]{:S(2)}) collective-permute-start(bf16[512,128]{1,0:T(8,128)(2,1)S(1)} %pack.1.rest_2_.refs_0_), channel_id=1, source_target_pairs={{0,8},{1,9},{2,10},{3,11},{4,12},{5,13},{6,14},{7,15},{8,0},{9,1},... | collective-permute-start | bytes 393224 | tf_op jit(solution)/shard_map/ppermute | solution.py:50
  5.0 7.1 %collective-permute-start.1 = (bf16[512,128]{1,0:T(8,128)(2,1)S(1)}, bf16[512,128]{1,0:T(8,128)(2,1)S(1)}, u32[]{:S(2)}, u32[]{:S(2)}) collective-permute-start(bf16[512,128]{1,0:T(8,128)(2,1)S(1)} %pack.1.rest_2_.refs_0_), channel_id=1, source_target_pairs={{0,4},{1,5},{2,6},{3,7},{4,0},{5,1},{6,2},{7,3},{8,12},{9,13},{10,... | collective-permute-start | bytes 393224 | tf_op jit(solution)/shard_map/ppermute | solution.py:50
  6.6 5.6 %collective-permute-start = (bf16[512,128]{1,0:T(8,128)(2,1)S(1)}, bf16[512,128]{1,0:T(8,128)(2,1)S(1)}, u32[]{:S(2)}, u32[]{:S(2)}) collective-permute-start(bf16[512,128]{1,0:T(8,128)(2,1)S(1)} %pack.1.rest_2_.refs_0_), channel_id=1, source_target_pairs={{0,2},{1,3},{2,0},{3,1},{4,6},{5,7},{6,4},{7,5},{8,10},{9,11},{10,... | collective-permute-start | bytes 393224 | tf_op jit(solution)/shard_map/ppermute | solution.py:50
  12.2 9.9 %collective-permute-start.4 = (bf16[768,128]{1,0:T(8,128)(2,1)S(1)}, bf16[768,128]{1,0:T(8,128)(2,1)S(1)}, u32[]{:S(2)}, u32[]{:S(2)}) collective-permute-start(bf16[768,128]{1,0:T(8,128)(2,1)S(1)} %merge.5), channel_id=1, source_target_pairs={{0,2},{1,3},{2,0},{3,1},{4,6},{5,7},{6,4},{7,5},{8,10},{9,11},{10,... | collective-permute-start | bytes 589832 | tf_op jit(solution)/shard_map/ppermute | solution.py:50
  13.3 8.9 %collective-permute-start.3 = (bf16[768,128]{1,0:T(8,128)(2,1)S(1)}, bf16[768,128]{1,0:T(8,128)(2,1)S(1)}, u32[]{:S(2)}, u32[]{:S(2)}) collective-permute-start(bf16[768,128]{1,0:T(8,128)(2,1)S(1)} %merge.4), channel_id=1, source_target_pairs={{0,4},{1,5},{2,6},{3,7},{4,0},{5,1},{6,2},{7,3},{8,12},{9,13},{10,... | collective-permute-start | bytes 589832 | tf_op jit(solution)/shard_map/ppermute | solution.py:50
  14.7 7.4 %collective-permute-start.5 = (bf16[512,128]{1,0:T(8,128)(2,1)S(1)}, bf16[512,128]{1,0:T(8,128)(2,1)S(1)}, u32[]{:S(2)}, u32[]{:S(2)}) collective-permute-start(bf16[512,128]{1,0:T(8,128)(2,1)S(1)} %collective-permute-done.2.refs_1_.rest_5_.refs_3_), channel_id=1, source_target_pairs={{0,6},{1,7},{2,4},{3,5},{4,2},{5,3},{6,0},{7,1},{8,14},{9,15},{10,... | collective-permute-start | bytes 393224 | tf_op jit(solution)/shard_map/ppermute | solution.py:50
  15.8 6.4 %collective-permute-start.6 = (bf16[2048,128]{1,0:T(8,128)(2,1)S(1)}, bf16[2048,128]{1,0:T(8,128)(2,1)S(1)}, u32[]{:S(2)}, u32[]{:S(2)}) collective-permute-start(bf16[2048,128]{1,0:T(8,128)(2,1)S(1)} %merge.6), channel_id=1, source_target_pairs={{0,1},{1,0},{2,3},{3,2},{4,5},{5,4},{6,7},{7,6},{8,9},{9,8},{10,11... | collective-permute-start | bytes 1572872 | tf_op jit(solution)/shard_map/ppermute | solution.py:50
  22.1 2.0 %collective-permute-start.7 = (bf16[2048,128]{1,0:T(8,128)(2,1)S(1)}, bf16[2048,128]{1,0:T(8,128)(2,1)S(1)}, u32[]{:S(2)}, u32[]{:S(2)}) collective-permute-start(bf16[2048,128]{1,0:T(8,128)(2,1)S(1)} %merge.7), channel_id=1, source_target_pairs={{0,1},{1,0},{2,3},{3,2},{4,5},{5,4},{6,7},{7,6},{8,9},{9,8},{10,11... | collective-permute-start | bytes 1572872 | tf_op jit(solution)/shard_map/ppermute | solution.py:50
  23.0 12.2 %copy-start = (bf16[1536,1024]{1,0:T(8,128)(2,1)S(1)}, bf16[1536,1024]{1,0:T(8,128)(2,1)}, u32[]{:S(2)}) copy-start(bf16[1536,1024]{1,0:T(8,128)(2,1)} %bank_ref.1) | copy-start | bytes 9437188
  23.0 12.1 %copy-start.1 = (s32[2]{0:T(128)S(1)}, s32[2]{0:T(128)}, u32[]{:S(2)}) copy-start(s32[2]{0:T(128)} %ids_ref.1) | copy-start | bytes 28

commit v4 on v3

--- a/solution.py
+++ b/solution.py
@@ -497,8 +497,8 @@
                     continue
                 if source or at > 2:
                     wanted[(at, by, 0), t] = (source, 0, 0), (at - source, by, 0)
-                elif at == 1 and t == 0:
-                    wanted[(at, by, 0), t] = (0, by, 0), (1, 0, 0)
+                elif at == 1:
+                    wanted[(at, by, 0), t] = (0, 0, 0), (1, by, 0)
                 else:
                     wanted[(at, by, 0), t] = (at, 0, 0), (0, by, 0)
     arrivals = []

time: 47.3 us -> 48.4 us (1.023)
  waiting for transfers between devices: 1.59 us -> 2.74 us
    ppermute x8, waiting for transfers between devices: 1.59 us -> 2.74 us  [moved(): return lax.ppermute(value, 'coord', pairs)]
  transfers between devices with their start and end apart: 8 -> 8, of which waited for: 2 -> 3; matrix products, arithmetic and copies ran while one was open for 0% -> 0% of each run, Pallas kernels for 22% -> 22%
where the time goes in v4:
time: 48.4 us; the launch traced here: 48.1 us
  blocking collectives  19.2 us (40%)
  Pallas kernels  15.2 us (31%)
  starting transfers between devices  10.9 us (23%)
  waiting for transfers between devices  2.74 us (6%)
    all_to_all x2, blocking collectives, exchanged(): lax.all_to_all(value, 'coord', split_axis=0, concat_axis=0, axis_index_gr...  19.2 us
    ppermute x8, starting transfers between devices, moved(): return lax.ppermute(value, 'coord', pairs)  10.9 us
    pallas_call x1, Pallas kernels, first_half(): pl.pallas_call(first_half_kernel, out_shape=jax.ShapeDtypeStruct((3, size...  4.03 us
    pallas_call x1, Pallas kernels, second_half(): pl.pallas_call(second_half_kernel, out_shape=jax.ShapeDtypeStruct((3, siz...  3.19 us
    ppermute x8, waiting for transfers between devices, moved(): return lax.ppermute(value, 'coord', pairs)  2.74 us
    pallas_call x1, Pallas kernels, project(): pl.pallas_call(functools.partial(project_kernel, n, early, seqs), out_sha...  2.51 us
    pallas_call x1, Pallas kernels, partial_scores(): pl.pallas_call(functools.partial(score_kernel, n), out_shape=jax.ShapeDty...  1.66 us
    pallas_call x1, Pallas kernels, whitened_blocks(): pl.pallas_call(functools.partial(whiten_kernel, n, seqs, late), out_shape...  1.23 us
  transfers between devices with their start and end apart: 8, of which 3 were waited for; matrix products, arithmetic and copies ran while one was open for 0% of the time, Pallas kernels for 22%

profile of v4, /device:TPU:0, one launch (start us, length us, event | category | flops | bytes accessed | tf_op | source)
XLA Modules:
  0.0 48.1 jit_solution(12809124149364676909)
XLA Ops:
  0.0 0.9 %pack.1.refs_0_.rest_2_ = bf16[512,128]{1,0:T(8,128)(2,1)S(1)} custom-call(bf16[256,128]{1,0:T(8,128)(2,1)} %first_hbm.1, bf16[256,128]{1,0:T(8,128)(2,1)} %second_hbm.1), custom_call_target="tpu_custom_call" | custom-call | tf_op jit(solution)/shard_map/pack/pallas_call | solution.py:79
  0.9 4.1 %collective-permute-start.2 = (bf16[512,128]{1,0:T(8,128)(2,1)S(1)}, bf16[512,128]{1,0:T(8,128)(2,1)S(1)}, u32[]{:S(2)}, u32[]{:S(2)}) collective-permute-start(bf16[512,128]{1,0:T(8,128)(2,1)S(1)} %pack.1.refs_0_.rest_2_), channel_id=1, source_target_pairs={{0,8},{1,9},{2,10},{3,11},{4,12},{5,13},{6,14},{7,15},{8,0},{9,1},... | collective-permute-start | bytes 393224 | tf_op jit(solution)/shard_map/ppermute | solution.py:50
  5.0 1.6 %collective-permute-start.1 = (bf16[512,128]{1,0:T(8,128)(2,1)S(1)}, bf16[512,128]{1,0:T(8,128)(2,1)S(1)}, u32[]{:S(2)}, u32[]{:S(2)}) collective-permute-start(bf16[512,128]{1,0:T(8,128)(2,1)S(1)} %pack.1.refs_0_.rest_2_), channel_id=1, source_target_pairs={{0,4},{1,5},{2,6},{3,7},{4,0},{5,1},{6,2},{7,3},{8,12},{9,13},{10,... | collective-permute-start | bytes 393224 | tf_op jit(solution)/shard_map/ppermute | solution.py:50
  6.6 1.5 %collective-permute-start = (bf16[512,128]{1,0:T(8,128)(2,1)S(1)}, bf16[512,128]{1,0:T(8,128)(2,1)S(1)}, u32[]{:S(2)}, u32[]{:S(2)}) collective-permute-start(bf16[512,128]{1,0:T(8,128)(2,1)S(1)} %pack.1.refs_0_.rest_2_), channel_id=1, source_target_pairs={{0,2},{1,3},{2,0},{3,1},{4,6},{5,7},{6,4},{7,5},{8,10},{9,11},{10,... | collective-permute-start | bytes 393224 | tf_op jit(solution)/shard_map/ppermute | solution.py:50
  8.1 4.0 %first_half.1.first_ref = f32[3,64,128]{2,1,0:T(8,128)S(1)} custom-call(f32[128,128]{1,0:T(8,128)} %cov_in_hbm.1, f32[128,128]{1,0:T(8,128)} %cov_out_hbm.1), custom_call_target="tpu_custom_call" | custom-call | flops 128 | bytes 128 | tf_op jit(solution)/shard_map/first_half/pallas_call | solution.py:201
  12.1 0.0 collective-permute-done.2.refs_1_.rest_5_.refs_3_
  12.1 0.0 collective-permute-done.1.rest_4_.refs_2_
  12.1 0.0 collective-permute-done.rest_3_.refs_1_
  12.2 1.9 %collective-permute-start.3 = (bf16[1024,128]{1,0:T(8,128)(2,1)S(1)}, bf16[1024,128]{1,0:T(8,128)(2,1)S(1)}, u32[]{:S(2)}, u32[]{:S(2)}) collective-permute-start(bf16[1024,128]{1,0:T(8,128)(2,1)S(1)} %merge.3), channel_id=1, source_target_pairs={{0,6},{1,7},{2,4},{3,5},{4,2},{5,3},{6,0},{7,1},{8,14},{9,15},{10,... | collective-permute-start | bytes 786440 | tf_op jit(solution)/shard_map/ppermute | solution.py:50
  14.1 0.6 %collective-permute-start.5 = (bf16[512,128]{1,0:T(8,128)(2,1)S(1)}, bf16[512,128]{1,0:T(8,128)(2,1)S(1)}, u32[]{:S(2)}, u32[]{:S(2)}) collective-permute-start(bf16[512,128]{1,0:T(8,128)(2,1)S(1)} %collective-permute-done.2.refs_1_.rest_5_.refs_3_), channel_id=1, source_target_pairs={{0,4},{1,5},{2,6},{3,7},{4,0},{5,1},{6,2},{7,3},{8,12},{9,13},{10,... | collective-permute-start | bytes 393224 | tf_op jit(solution)/shard_map/ppermute | solution.py:50
  14.7 1.0 %collective-permute-start.4 = (bf16[512,128]{1,0:T(8,128)(2,1)S(1)}, bf16[512,128]{1,0:T(8,128)(2,1)S(1)}, u32[]{:S(2)}, u32[]{:S(2)}) collective-permute-start(bf16[512,128]{1,0:T(8,128)(2,1)S(1)} %collective-permute-done.2.refs_1_.rest_5_.refs_3_), channel_id=1, source_target_pairs={{0,2},{1,3},{2,0},{3,1},{4,6},{5,7},{6,4},{7,5},{8,10},{9,11},{10,... | collective-permute-start | bytes 393224 | tf_op jit(solution)/shard_map/ppermute | solution.py:50
  15.8 0.1 collective-permute-start.6
  15.8 3.2 %second_half.1.k_ref = f32[3,128,128]{2,1,0:T(8,128)S(1)} custom-call(f32[3,64,128]{2,1,0:T(8,128)S(1)} %first_half.1.first_ref, s32[2]{0:T(128)} %len_hbm.1), custom_call_target="tpu_custom_call" | custom-call | flops 128 | bytes 128 | tf_op jit(solution)/shard_map/second_half/pallas_call | solution.py:215
  19.0 2.5 %project.1 = (f32[2,256,128]{2,1,0:T(8,128)S(1)}, bf16[2,256,4096]{2,1,0:T(8,128)(2,1)S(1)}) custom-call(s32[1]{0:T(128)} %bitcast.me_ref, bf16[256,4096]{1,0:T(8,128)(2,1)} %bitcast.3, bf16[256,4096]{1,0:T(8,128)(2,1)} %bitcast.4, bf16[512,128]{1,0:T(8,128)(2,1)S(1)} %pack.1.refs_0_.rest_2_, bf16[512,128]{1,0:T(8,128)(2,1)S(1)} %collective-permute-done.rest_3_.refs_1_, ...), custom_call_target="tpu_custom_call" | custom-call | flops 128 | bytes 128 | tf_op jit(solution)/shard_map/project/pallas_call | solution.py:318
  21.6 0.7 %collective-permute-done.5.rest_3_.refs_2_ = bf16[512,128]{1,0:T(8,128)(2,1)S(1)} collective-permute-done((bf16[512,128]{1,0:T(8,128)(2,1)S(1)}, bf16[512,128]{1,0:T(8,128)(2,1)S(1)}, u32[]{:S(2)}, u32[]{:S(2)}) %collective-permute-start.5) | collective-permute-done | bytes 131104 | tf_op jit(solution)/shard_map/ppermute | solution.py:50
  22.2 0.9 %collective-permute-done.4.rest_2_.refs_1_ = bf16[512,128]{1,0:T(8,128)(2,1)S(1)} collective-permute-done((bf16[512,128]{1,0:T(8,128)(2,1)S(1)}, bf16[512,128]{1,0:T(8,128)(2,1)S(1)}, u32[]{:S(2)}, u32[]{:S(2)}) %collective-permute-start.4) | collective-permute-done | bytes 131104 | tf_op jit(solution)/shard_map/ppermute | solution.py:50
  23.1 0.0 collective-permute-done.3.rest_1_.refs_0_
  23.2 0.1 collective-permute-start.7
  23.3 0.0 collective-permute-done.6.rest_0_
  23.3 0.7 %extend.1.total_ref = f32[2,256,128]{2,1,0:T(8,128)S(1)} custom-call(s32[1]{0:T(128)} %bitcast.me_ref, f32[2,256,128]{2,1,0:T(8,128)S(1)} %get-tuple-element.23.total_ref, bf16[2,256,4096]{2,1,0:T(8,128)(2,1)S(1)} %get-tuple-element.24.held.rest_0_, bf16[2048,128]{1,0:T(8,128)(2,1)S(1)} %collective-permute-done.6.rest_0_, ...), custom_call_target="tpu_custom_call" | custom-call | flops 65536 | bytes 65536 | tf_op jit(solution)/shard_map/extend/pallas_call | solution.py:349
  24.0 0.0 copy-start
  24.0 0.0 copy-start.1
  24.0 1.1 %collective-permute-done.7.rest_1_ = bf16[2048,128]{1,0:T(8,128)(2,1)S(1)} collective-permute-done((bf16[2048,128]{1,0:T(8,128)(2,1)S(1)}, bf16[2048,128]{1,0:T(8,128)(2,1)S(1)}, u32[]{:S(2)}, u32[]{:S(2)}) %collective-permute-start.7) | collective-permute-done | bytes 524320 | tf_op jit(solution)/shard_map/ppermute | solution.py:50
  25.2 1.2 %whiten.1 = bf16[16,16,128]{2,1,0:T(8,128)(2,1)S(1)} custom-call(s32[1]{0:T(128)} %bitcast.me_ref, f32[2,256,128]{2,1,0:T(8,128)S(1)} %extend.1.total_ref, f32[3,128,128]{2,1,0:T(8,128)S(1)} %second_half.1.k_ref, bf16[2,256,4096]{2,1,0:T(8,128)(2,1)S(1)} %get-tuple-element.24.held.rest_0_, bf16[2048,128]{1,0:T(8,128)(2,1)S(1)} %collective-permute-done.7.rest_1_), custom_call_target="tpu_custom_call" | custom-call | flops 134217728 | bytes 4194304 | tf_op jit(solution)/shard_map/whiten/pallas_call | solution.py:391
  26.4 9.8 %all_to_all.10.white_ref = bf16[16,16,128]{2,1,0:T(8,128)(2,1)S(1)} all-to-all(bf16[16,16,128]{2,1,0:T(8,128)(2,1)S(1)} %whiten.1), channel_id=1, replica_groups={{11,9,7,5,15,13,3,1,10,8,6,4,14,12,2,0},{27,25,23,21,31,29,19,17,26,24,..., dimensions={0} | all-to-all | bytes 131072 | tf_op jit(solution)/shard_map/all_to_all | solution.py:405
  36.2 0.0 copy-done
  36.2 0.0 copy-done.1
  36.2 1.7 %score.1 = bf16[16,32,128]{2,1,0:T(8,128)(2,1)S(1)} custom-call(s32[1]{0:T(128)} %bitcast.me_ref, s32[2]{0:T(128)S(1)} %copy-done.1, bf16[16,16,128]{2,1,0:T(8,128)(2,1)S(1)} %all_to_all.10.white_ref, bf16[1536,1024]{1,0:T(8,128)(2,1)S(1)} %copy-done), custom_call_target="tpu_custom_call" | custom-call | flops 100663296 | bytes 3145728 | tf_op jit(solution)/shard_map/score/pallas_call | solution.py:437
  37.9 9.4 %all_to_all.11.a = bf16[16,32,128]{2,1,0:T(8,128)(2,1)S(1)} all-to-all(bf16[16,32,128]{2,1,0:T(8,128)(2,1)S(1)} %score.1), channel_id=1, replica_groups={{11,9,7,5,15,13,3,1,10,8,6,4,14,12,2,0},{27,25,23,21,31,29,19,17,26,24,..., dimensions={0} | all-to-all | bytes 262144 | tf_op jit(solution)/shard_map/all_to_all | solution.py:405
  47.3 0.9 %place.1 = bf16[32,96]{1,0:T(8,128)(2,1)} custom-call(bf16[16,32,128]{2,1,0:T(8,128)(2,1)S(1)} %all_to_all.11.a), custom_call_target="tpu_custom_call" | custom-call | tf_op jit(solution)/shard_map/place/pallas_call | solution.py:463
  (3 shorter events, 0.1 us)
Async XLA Ops:
  0.9 11.2 %collective-permute-start.2 = (bf16[512,128]{1,0:T(8,128)(2,1)S(1)}, bf16[512,128]{1,0:T(8,128)(2,1)S(1)}, u32[]{:S(2)}, u32[]{:S(2)}) collective-permute-start(bf16[512,128]{1,0:T(8,128)(2,1)S(1)} %pack.1.refs_0_.rest_2_), channel_id=1, source_target_pairs={{0,8},{1,9},{2,10},{3,11},{4,12},{5,13},{6,14},{7,15},{8,0},{9,1},... | collective-permute-start | bytes 393224 | tf_op jit(solution)/shard_map/ppermute | solution.py:50
  5.0 7.1 %collective-permute-start.1 = (bf16[512,128]{1,0:T(8,128)(2,1)S(1)}, bf16[512,128]{1,0:T(8,128)(2,1)S(1)}, u32[]{:S(2)}, u32[]{:S(2)}) collective-permute-start(bf16[512,128]{1,0:T(8,128)(2,1)S(1)} %pack.1.refs_0_.rest_2_), channel_id=1, source_target_pairs={{0,4},{1,5},{2,6},{3,7},{4,0},{5,1},{6,2},{7,3},{8,12},{9,13},{10,... | collective-permute-start | bytes 393224 | tf_op jit(solution)/shard_map/ppermute | solution.py:50
  6.6 5.6 %collective-permute-start = (bf16[512,128]{1,0:T(8,128)(2,1)S(1)}, bf16[512,128]{1,0:T(8,128)(2,1)S(1)}, u32[]{:S(2)}, u32[]{:S(2)}) collective-permute-start(bf16[512,128]{1,0:T(8,128)(2,1)S(1)} %pack.1.refs_0_.rest_2_), channel_id=1, source_target_pairs={{0,2},{1,3},{2,0},{3,1},{4,6},{5,7},{6,4},{7,5},{8,10},{9,11},{10,... | collective-permute-start | bytes 393224 | tf_op jit(solution)/shard_map/ppermute | solution.py:50
  12.2 11.0 %collective-permute-start.3 = (bf16[1024,128]{1,0:T(8,128)(2,1)S(1)}, bf16[1024,128]{1,0:T(8,128)(2,1)S(1)}, u32[]{:S(2)}, u32[]{:S(2)}) collective-permute-start(bf16[1024,128]{1,0:T(8,128)(2,1)S(1)} %merge.3), channel_id=1, source_target_pairs={{0,6},{1,7},{2,4},{3,5},{4,2},{5,3},{6,0},{7,1},{8,14},{9,15},{10,... | collective-permute-start | bytes 786440 | tf_op jit(solution)/shard_map/ppermute | solution.py:50
  14.1 8.2 %collective-permute-start.5 = (bf16[512,128]{1,0:T(8,128)(2,1)S(1)}, bf16[512,128]{1,0:T(8,128)(2,1)S(1)}, u32[]{:S(2)}, u32[]{:S(2)}) collective-permute-start(bf16[512,128]{1,0:T(8,128)(2,1)S(1)} %collective-permute-done.2.refs_1_.rest_5_.refs_3_), channel_id=1, source_target_pairs={{0,4},{1,5},{2,6},{3,7},{4,0},{5,1},{6,2},{7,3},{8,12},{9,13},{10,... | collective-permute-start | bytes 393224 | tf_op jit(solution)/shard_map/ppermute | solution.py:50
  14.7 8.4 %collective-permute-start.4 = (bf16[512,128]{1,0:T(8,128)(2,1)S(1)}, bf16[512,128]{1,0:T(8,128)(2,1)S(1)}, u32[]{:S(2)}, u32[]{:S(2)}) collective-permute-start(bf16[512,128]{1,0:T(8,128)(2,1)S(1)} %collective-permute-done.2.refs_1_.rest_5_.refs_3_), channel_id=1, source_target_pairs={{0,2},{1,3},{2,0},{3,1},{4,6},{5,7},{6,4},{7,5},{8,10},{9,11},{10,... | collective-permute-start | bytes 393224 | tf_op jit(solution)/shard_map/ppermute | solution.py:50
  15.8 7.5 %collective-permute-start.6 = (bf16[2048,128]{1,0:T(8,128)(2,1)S(1)}, bf16[2048,128]{1,0:T(8,128)(2,1)S(1)}, u32[]{:S(2)}, u32[]{:S(2)}) collective-permute-start(bf16[2048,128]{1,0:T(8,128)(2,1)S(1)} %merge.4), channel_id=1, source_target_pairs={{0,1},{1,0},{2,3},{3,2},{4,5},{5,4},{6,7},{7,6},{8,9},{9,8},{10,11... | collective-permute-start | bytes 1572872 | tf_op jit(solution)/shard_map/ppermute | solution.py:50
  23.2 2.0 %collective-permute-start.7 = (bf16[2048,128]{1,0:T(8,128)(2,1)S(1)}, bf16[2048,128]{1,0:T(8,128)(2,1)S(1)}, u32[]{:S(2)}, u32[]{:S(2)}) collective-permute-start(bf16[2048,128]{1,0:T(8,128)(2,1)S(1)} %merge.5), channel_id=1, source_target_pairs={{0,1},{1,0},{2,3},{3,2},{4,5},{5,4},{6,7},{7,6},{8,9},{9,8},{10,11... | collective-permute-start | bytes 1572872 | tf_op jit(solution)/shard_map/ppermute | solution.py:50
  24.0 12.2 %copy-start = (bf16[1536,1024]{1,0:T(8,128)(2,1)S(1)}, bf16[1536,1024]{1,0:T(8,128)(2,1)}, u32[]{:S(2)}) copy-start(bf16[1536,1024]{1,0:T(8,128)(2,1)} %bank_ref.1) | copy-start | bytes 9437188
  24.0 12.2 %copy-start.1 = (s32[2]{0:T(128)S(1)}, s32[2]{0:T(128)}, u32[]{:S(2)}) copy-start(s32[2]{0:T(128)} %ids_ref.1) | copy-start | bytes 28

commit v5 on v3

--- a/solution.py
+++ b/solution.py
@@ -52,7 +52,7 @@
 
 def exchange_order(n):
     a, b, c = factors(n)
-    return sorted(range(n), key=lambda device: (1 - device % 2, abs(2 * (device // (b * c)) - (a - 1)), -device))
+    return sorted(range(n), key=lambda device: (abs(2 * (device // (b * c)) - (a - 1)), 1 - device % 2, -device))
 
 
 def place_of(me, n):

time: 47.3 us -> 47.3 us (level)
  no operation moved by 1% of the time
where the time goes in v5:
time: 47.3 us; the launch traced here: 47 us
  blocking collectives  19.1 us (40%)
  Pallas kernels  15.2 us (32%)
  starting transfers between devices  11 us (23%)
  waiting for transfers between devices  1.59 us (3%)
    all_to_all x2, blocking collectives, exchanged(): lax.all_to_all(value, 'coord', split_axis=0, concat_axis=0, axis_index_gr...  19.1 us
    ppermute x8, starting transfers between devices, moved(): return lax.ppermute(value, 'coord', pairs)  11 us
    pallas_call x1, Pallas kernels, first_half(): pl.pallas_call(first_half_kernel, out_shape=jax.ShapeDtypeStruct((3, size...  4.03 us
    pallas_call x1, Pallas kernels, second_half(): pl.pallas_call(second_half_kernel, out_shape=jax.ShapeDtypeStruct((3, siz...  3.19 us
    pallas_call x1, Pallas kernels, project(): pl.pallas_call(functools.partial(project_kernel, n, early, seqs), out_sha...  2.51 us
    pallas_call x1, Pallas kernels, partial_scores(): pl.pallas_call(functools.partial(score_kernel, n), out_shape=jax.ShapeDty...  1.66 us
    ppermute x8, waiting for transfers between devices, moved(): return lax.ppermute(value, 'coord', pairs)  1.59 us
    pallas_call x1, Pallas kernels, whitened_blocks(): pl.pallas_call(functools.partial(whiten_kernel, n, seqs, late), out_shape...  1.23 us
  transfers between devices with their start and end apart: 8, of which 2 were waited for; matrix products, arithmetic and copies ran while one was open for 0% of the time, Pallas kernels for 22%

profile of v5, /device:TPU:0, one launch (start us, length us, event | category | flops | bytes accessed | tf_op | source)
XLA Modules:
  0.0 47.0 jit_solution(18255586870402438196)
XLA Ops:
  0.0 0.9 %pack.1.rest_2_.refs_0_ = bf16[512,128]{1,0:T(8,128)(2,1)S(1)} custom-call(bf16[256,128]{1,0:T(8,128)(2,1)} %first_hbm.1, bf16[256,128]{1,0:T(8,128)(2,1)} %second_hbm.1), custom_call_target="tpu_custom_call" | custom-call | tf_op jit(solution)/shard_map/pack/pallas_call | solution.py:79
  0.9 4.1 %collective-permute-start.2 = (bf16[512,128]{1,0:T(8,128)(2,1)S(1)}, bf16[512,128]{1,0:T(8,128)(2,1)S(1)}, u32[]{:S(2)}, u32[]{:S(2)}) collective-permute-start(bf16[512,128]{1,0:T(8,128)(2,1)S(1)} %pack.1.rest_2_.refs_0_), channel_id=1, source_target_pairs={{0,8},{1,9},{2,10},{3,11},{4,12},{5,13},{6,14},{7,15},{8,0},{9,1},... | collective-permute-start | bytes 393224 | tf_op jit(solution)/shard_map/ppermute | solution.py:50
  5.0 1.6 %collective-permute-start.1 = (bf16[512,128]{1,0:T(8,128)(2,1)S(1)}, bf16[512,128]{1,0:T(8,128)(2,1)S(1)}, u32[]{:S(2)}, u32[]{:S(2)}) collective-permute-start(bf16[512,128]{1,0:T(8,128)(2,1)S(1)} %pack.1.rest_2_.refs_0_), channel_id=1, source_target_pairs={{0,4},{1,5},{2,6},{3,7},{4,0},{5,1},{6,2},{7,3},{8,12},{9,13},{10,... | collective-permute-start | bytes 393224 | tf_op jit(solution)/shard_map/ppermute | solution.py:50
  6.6 1.5 %collective-permute-start = (bf16[512,128]{1,0:T(8,128)(2,1)S(1)}, bf16[512,128]{1,0:T(8,128)(2,1)S(1)}, u32[]{:S(2)}, u32[]{:S(2)}) collective-permute-start(bf16[512,128]{1,0:T(8,128)(2,1)S(1)} %pack.1.rest_2_.refs_0_), channel_id=1, source_target_pairs={{0,2},{1,3},{2,0},{3,1},{4,6},{5,7},{6,4},{7,5},{8,10},{9,11},{10,... | collective-permute-start | bytes 393224 | tf_op jit(solution)/shard_map/ppermute | solution.py:50
  8.1 4.0 %first_half.1.first_ref = f32[3,64,128]{2,1,0:T(8,128)S(1)} custom-call(f32[128,128]{1,0:T(8,128)} %cov_in_hbm.1, f32[128,128]{1,0:T(8,128)} %cov_out_hbm.1), custom_call_target="tpu_custom_call" | custom-call | flops 128 | bytes 128 | tf_op jit(solution)/shard_map/first_half/pallas_call | solution.py:201
  12.1 0.0 collective-permute-done.2.refs_1_.rest_5_.refs_3_
  12.1 0.0 collective-permute-done.1.refs_0_.rest_4_.refs_2_
  12.1 0.0 collective-permute-done.refs_0_.rest_3_.refs_1_
  12.2 1.1 %collective-permute-start.4 = (bf16[768,128]{1,0:T(8,128)(2,1)S(1)}, bf16[768,128]{1,0:T(8,128)(2,1)S(1)}, u32[]{:S(2)}, u32[]{:S(2)}) collective-permute-start(bf16[768,128]{1,0:T(8,128)(2,1)S(1)} %merge.5), channel_id=1, source_target_pairs={{0,2},{1,3},{2,0},{3,1},{4,6},{5,7},{6,4},{7,5},{8,10},{9,11},{10,... | collective-permute-start | bytes 589832 | tf_op jit(solution)/shard_map/ppermute | solution.py:50
  13.3 1.5 %collective-permute-start.3 = (bf16[768,128]{1,0:T(8,128)(2,1)S(1)}, bf16[768,128]{1,0:T(8,128)(2,1)S(1)}, u32[]{:S(2)}, u32[]{:S(2)}) collective-permute-start(bf16[768,128]{1,0:T(8,128)(2,1)S(1)} %merge.4), channel_id=1, source_target_pairs={{0,4},{1,5},{2,6},{3,7},{4,0},{5,1},{6,2},{7,3},{8,12},{9,13},{10,... | collective-permute-start | bytes 589832 | tf_op jit(solution)/shard_map/ppermute | solution.py:50
  14.7 1.1 %collective-permute-start.5 = (bf16[512,128]{1,0:T(8,128)(2,1)S(1)}, bf16[512,128]{1,0:T(8,128)(2,1)S(1)}, u32[]{:S(2)}, u32[]{:S(2)}) collective-permute-start(bf16[512,128]{1,0:T(8,128)(2,1)S(1)} %collective-permute-done.2.refs_1_.rest_5_.refs_3_), channel_id=1, source_target_pairs={{0,6},{1,7},{2,4},{3,5},{4,2},{5,3},{6,0},{7,1},{8,14},{9,15},{10,... | collective-permute-start | bytes 393224 | tf_op jit(solution)/shard_map/ppermute | solution.py:50
  15.8 0.1 collective-permute-start.6
  15.9 3.2 %second_half.1.k_ref = f32[3,128,128]{2,1,0:T(8,128)S(1)} custom-call(f32[3,64,128]{2,1,0:T(8,128)S(1)} %first_half.1.first_ref, s32[2]{0:T(128)} %len_hbm.1), custom_call_target="tpu_custom_call" | custom-call | flops 128 | bytes 128 | tf_op jit(solution)/shard_map/second_half/pallas_call | solution.py:215
  19.1 2.5 %project.1 = (f32[2,256,128]{2,1,0:T(8,128)S(1)}, bf16[2,256,4096]{2,1,0:T(8,128)(2,1)S(1)}) custom-call(s32[1]{0:T(128)} %bitcast.me_ref, bf16[256,4096]{1,0:T(8,128)(2,1)} %bitcast.3, bf16[256,4096]{1,0:T(8,128)(2,1)} %bitcast.4, bf16[512,128]{1,0:T(8,128)(2,1)S(1)} %pack.1.rest_2_.refs_0_, ...), custom_call_target="tpu_custom_call" | custom-call | flops 128 | bytes 128 | tf_op jit(solution)/shard_map/project/pallas_call | solution.py:318
  21.6 0.5 collective-permute-done.5.rest_3_.refs_2_
  22.1 0.0 collective-permute-done.4.rest_2_.refs_1_
  22.1 0.0 collective-permute-done.3.rest_1_.refs_0_
  22.1 0.1 collective-permute-start.7
  22.3 0.0 collective-permute-done.6.rest_0_
  22.3 0.7 %extend.1.total_ref = f32[2,256,128]{2,1,0:T(8,128)S(1)} custom-call(s32[1]{0:T(128)} %bitcast.me_ref, f32[2,256,128]{2,1,0:T(8,128)S(1)} %get-tuple-element.23.total_ref, bf16[2,256,4096]{2,1,0:T(8,128)(2,1)S(1)} %get-tuple-element.24.held.rest_0_, bf16[2048,128]{1,0:T(8,128)(2,1)S(1)} %collective-permute-done.6.rest_0_, ...), custom_call_target="tpu_custom_call" | custom-call | flops 65536 | bytes 65536 | tf_op jit(solution)/shard_map/extend/pallas_call | solution.py:349
  23.0 0.0 copy-start
  23.0 0.0 copy-start.1
  23.0 1.1 %collective-permute-done.7.rest_1_ = bf16[2048,128]{1,0:T(8,128)(2,1)S(1)} collective-permute-done((bf16[2048,128]{1,0:T(8,128)(2,1)S(1)}, bf16[2048,128]{1,0:T(8,128)(2,1)S(1)}, u32[]{:S(2)}, u32[]{:S(2)}) %collective-permute-start.7) | collective-permute-done | bytes 524320 | tf_op jit(solution)/shard_map/ppermute | solution.py:50
  24.1 1.2 %whiten.1 = bf16[16,16,128]{2,1,0:T(8,128)(2,1)S(1)} custom-call(s32[1]{0:T(128)} %bitcast.me_ref, f32[2,256,128]{2,1,0:T(8,128)S(1)} %extend.1.total_ref, f32[3,128,128]{2,1,0:T(8,128)S(1)} %second_half.1.k_ref, bf16[2,256,4096]{2,1,0:T(8,128)(2,1)S(1)} %get-tuple-element.24.held.rest_0_, bf16[2048,128]{1,0:T(8,128)(2,1)S(1)} %collective-permute-done.7.rest_1_), custom_call_target="tpu_custom_call" | custom-call | flops 134217728 | bytes 4194304 | tf_op jit(solution)/shard_map/whiten/pallas_call | solution.py:391
  25.4 9.8 %all_to_all.10.white_ref = bf16[16,16,128]{2,1,0:T(8,128)(2,1)S(1)} all-to-all(bf16[16,16,128]{2,1,0:T(8,128)(2,1)S(1)} %whiten.1), channel_id=1, replica_groups={{11,9,7,5,10,8,6,4,15,13,3,1,14,12,2,0},{27,25,23,21,26,24,22,20,31,29,..., dimensions={0} | all-to-all | bytes 131072 | tf_op jit(solution)/shard_map/all_to_all | solution.py:405
  35.1 0.0 copy-done
  35.1 0.0 copy-done.1
  35.2 1.7 %score.1 = bf16[16,32,128]{2,1,0:T(8,128)(2,1)S(1)} custom-call(s32[1]{0:T(128)} %bitcast.me_ref, s32[2]{0:T(128)S(1)} %copy-done.1, bf16[16,16,128]{2,1,0:T(8,128)(2,1)S(1)} %all_to_all.10.white_ref, bf16[1536,1024]{1,0:T(8,128)(2,1)S(1)} %copy-done), custom_call_target="tpu_custom_call" | custom-call | flops 100663296 | bytes 3145728 | tf_op jit(solution)/shard_map/score/pallas_call | solution.py:437
  36.8 9.4 %all_to_all.11.a = bf16[16,32,128]{2,1,0:T(8,128)(2,1)S(1)} all-to-all(bf16[16,32,128]{2,1,0:T(8,128)(2,1)S(1)} %score.1), channel_id=1, replica_groups={{11,9,7,5,10,8,6,4,15,13,3,1,14,12,2,0},{27,25,23,21,26,24,22,20,31,29,..., dimensions={0} | all-to-all | bytes 262144 | tf_op jit(solution)/shard_map/all_to_all | solution.py:405
  46.2 0.9 %place.1 = bf16[32,96]{1,0:T(8,128)(2,1)} custom-call(bf16[16,32,128]{2,1,0:T(8,128)(2,1)S(1)} %all_to_all.11.a), custom_call_target="tpu_custom_call" | custom-call | tf_op jit(solution)/shard_map/place/pallas_call | solution.py:463
  (4 shorter events, 0.1 us)
Async XLA Ops:
  0.9 11.2 %collective-permute-start.2 = (bf16[512,128]{1,0:T(8,128)(2,1)S(1)}, bf16[512,128]{1,0:T(8,128)(2,1)S(1)}, u32[]{:S(2)}, u32[]{:S(2)}) collective-permute-start(bf16[512,128]{1,0:T(8,128)(2,1)S(1)} %pack.1.rest_2_.refs_0_), channel_id=1, source_target_pairs={{0,8},{1,9},{2,10},{3,11},{4,12},{5,13},{6,14},{7,15},{8,0},{9,1},... | collective-permute-start | bytes 393224 | tf_op jit(solution)/shard_map/ppermute | solution.py:50
  5.0 7.1 %collective-permute-start.1 = (bf16[512,128]{1,0:T(8,128)(2,1)S(1)}, bf16[512,128]{1,0:T(8,128)(2,1)S(1)}, u32[]{:S(2)}, u32[]{:S(2)}) collective-permute-start(bf16[512,128]{1,0:T(8,128)(2,1)S(1)} %pack.1.rest_2_.refs_0_), channel_id=1, source_target_pairs={{0,4},{1,5},{2,6},{3,7},{4,0},{5,1},{6,2},{7,3},{8,12},{9,13},{10,... | collective-permute-start | bytes 393224 | tf_op jit(solution)/shard_map/ppermute | solution.py:50
  6.6 5.6 %collective-permute-start = (bf16[512,128]{1,0:T(8,128)(2,1)S(1)}, bf16[512,128]{1,0:T(8,128)(2,1)S(1)}, u32[]{:S(2)}, u32[]{:S(2)}) collective-permute-start(bf16[512,128]{1,0:T(8,128)(2,1)S(1)} %pack.1.rest_2_.refs_0_), channel_id=1, source_target_pairs={{0,2},{1,3},{2,0},{3,1},{4,6},{5,7},{6,4},{7,5},{8,10},{9,11},{10,... | collective-permute-start | bytes 393224 | tf_op jit(solution)/shard_map/ppermute | solution.py:50
  12.2 9.9 %collective-permute-start.4 = (bf16[768,128]{1,0:T(8,128)(2,1)S(1)}, bf16[768,128]{1,0:T(8,128)(2,1)S(1)}, u32[]{:S(2)}, u32[]{:S(2)}) collective-permute-start(bf16[768,128]{1,0:T(8,128)(2,1)S(1)} %merge.5), channel_id=1, source_target_pairs={{0,2},{1,3},{2,0},{3,1},{4,6},{5,7},{6,4},{7,5},{8,10},{9,11},{10,... | collective-permute-start | bytes 589832 | tf_op jit(solution)/shard_map/ppermute | solution.py:50
  13.3 8.9 %collective-permute-start.3 = (bf16[768,128]{1,0:T(8,128)(2,1)S(1)}, bf16[768,128]{1,0:T(8,128)(2,1)S(1)}, u32[]{:S(2)}, u32[]{:S(2)}) collective-permute-start(bf16[768,128]{1,0:T(8,128)(2,1)S(1)} %merge.4), channel_id=1, source_target_pairs={{0,4},{1,5},{2,6},{3,7},{4,0},{5,1},{6,2},{7,3},{8,12},{9,13},{10,... | collective-permute-start | bytes 589832 | tf_op jit(solution)/shard_map/ppermute | solution.py:50
  14.7 7.4 %collective-permute-start.5 = (bf16[512,128]{1,0:T(8,128)(2,1)S(1)}, bf16[512,128]{1,0:T(8,128)(2,1)S(1)}, u32[]{:S(2)}, u32[]{:S(2)}) collective-permute-start(bf16[512,128]{1,0:T(8,128)(2,1)S(1)} %collective-permute-done.2.refs_1_.rest_5_.refs_3_), channel_id=1, source_target_pairs={{0,6},{1,7},{2,4},{3,5},{4,2},{5,3},{6,0},{7,1},{8,14},{9,15},{10,... | collective-permute-start | bytes 393224 | tf_op jit(solution)/shard_map/ppermute | solution.py:50
  15.8 6.4 %collective-permute-start.6 = (bf16[2048,128]{1,0:T(8,128)(2,1)S(1)}, bf16[2048,128]{1,0:T(8,128)(2,1)S(1)}, u32[]{:S(2)}, u32[]{:S(2)}) collective-permute-start(bf16[2048,128]{1,0:T(8,128)(2,1)S(1)} %merge.6), channel_id=1, source_target_pairs={{0,1},{1,0},{2,3},{3,2},{4,5},{5,4},{6,7},{7,6},{8,9},{9,8},{10,11... | collective-permute-start | bytes 1572872 | tf_op jit(solution)/shard_map/ppermute | solution.py:50
  22.1 2.0 %collective-permute-start.7 = (bf16[2048,128]{1,0:T(8,128)(2,1)S(1)}, bf16[2048,128]{1,0:T(8,128)(2,1)S(1)}, u32[]{:S(2)}, u32[]{:S(2)}) collective-permute-start(bf16[2048,128]{1,0:T(8,128)(2,1)S(1)} %merge.7), channel_id=1, source_target_pairs={{0,1},{1,0},{2,3},{3,2},{4,5},{5,4},{6,7},{7,6},{8,9},{9,8},{10,11... | collective-permute-start | bytes 1572872 | tf_op jit(solution)/shard_map/ppermute | solution.py:50
  23.0 12.2 %copy-start = (bf16[1536,1024]{1,0:T(8,128)(2,1)S(1)}, bf16[1536,1024]{1,0:T(8,128)(2,1)}, u32[]{:S(2)}) copy-start(bf16[1536,1024]{1,0:T(8,128)(2,1)} %bank_ref.1) | copy-start | bytes 9437188
  23.0 12.1 %copy-start.1 = (s32[2]{0:T(128)S(1)}, s32[2]{0:T(128)}, u32[]{:S(2)}) copy-start(s32[2]{0:T(128)} %ids_ref.1) | copy-start | bytes 28
